TPU v7x, 128 devices: a whole 4x4x4 slice. The times are simulated.
128 devices in a mesh: row: 16 (over z, y_hi, core), col: 8 (over y_lo, x).
Axes of the slice: x: 4, y: 4 (y_hi: 2, y_lo: 2; y = y_hi * 2 + y_lo), z: 4, core: 2. Of those that a mesh axis runs over, the one named last changes fastest.
Arguments:
- demand: float32 [4096, 8192], P('row', 'col'), may hold values from 0.2 to 2
- leakage: float32 [4096, 8192], P('row', 'col'), may hold values from 0.05 to 0.5
- conductance: float32 [4096, 8192], P('row', 'col'), may hold values from 0.5 to 4
- vias: int32 [4096, 8192], P('row', 'col'), may hold values 0 or 1
- layer_of: int32 [512, 1024], P('row'), may hold values from 0 to 63
- lateral_k: float32 [64, 512, 1024], P('col', 'row'), may hold values from 0.3 to 3
- vertical_k: float32 [64, 512, 1024], P('col', 'row'), may hold values from 0.1 to 1
Outputs:
- drop: float32 [4096, 8192], P('row', 'col')
- temperature: float32 [64, 512, 1024], P('col', 'row')
All inputs are finite; a program needn't handle non-finite values. No bound on the sum of `vias` on one device may be relied on, other than what follows from the above.
Results may differ from a plain program's by a relative error of at most 0.0001.
Values sent between devices are 32-bit elements; how exact they have to be, the bound alone decides.
A program may use at most 128 MiB of HBM per device.

v0:
```python
import jax
import jax.numpy as jnp
from jax import lax
from jax.sharding import PartitionSpec as P

COARSE = 8
SWEEPS = 4
HEAT_SWEEPS = 4
OUTER = 2


COND_SLOPE = 0.5
LEAK_SLOPE = 0.7
VIA_CONDUCT = 4.0


def extended(block, sides, width):
    for axis, dim in sides:
        count = lax.axis_size(axis)
        forward = [(i, i + 1) for i in range(count - 1)]
        backward = [(target, source) for source, target in forward]
        low = lax.ppermute(
            lax.slice_in_dim(block, block.shape[dim] - width, None, axis=dim), axis, forward
        )
        high = lax.ppermute(lax.slice_in_dim(block, 0, width, axis=dim), axis, backward)
        block = jnp.concatenate([low, block, high], axis=dim)
    return block


def fine_of(coarse):
    count_rows, count_cols = coarse.shape
    spread = jnp.broadcast_to(coarse[:, None, :, None], (count_rows, COARSE, count_cols, COARSE))
    return spread.reshape(count_rows * COARSE, count_cols * COARSE)


def coarse_of(fine):
    count_rows = fine.shape[0] // COARSE
    count_cols = fine.shape[1] // COARSE
    return jnp.mean(fine.reshape(count_rows, COARSE, count_cols, COARSE), axis=(1, 3))


def edge_weights(cond_ext):
    center = cond_ext[1:-1, 1:-1]
    w_north = (center + cond_ext[:-2, 1:-1]) * 0.5
    w_south = (center + cond_ext[2:, 1:-1]) * 0.5
    w_west = (center + cond_ext[1:-1, :-2]) * 0.5
    w_east = (center + cond_ext[1:-1, 2:]) * 0.5
    return (w_north, w_south, w_west, w_east)


def neighbour_sum(load, weights, drop_ext):
    w_north, w_south, w_west, w_east = weights
    return (
        load
        + w_north * drop_ext[:-2, 1:-1]
        + w_south * drop_ext[2:, 1:-1]
        + w_west * drop_ext[1:-1, :-2]
        + w_east * drop_ext[1:-1, 2:]
    )


def power_phase(drop, cond, load, via_g):
    cond_ext = extended(cond, (("row", 0), ("col", 1)), 1)
    weights = edge_weights(cond_ext)
    denom = weights[0] + weights[1] + weights[2] + weights[3] + via_g
    for sweep in range(SWEEPS):
        drop_ext = extended(drop, (("row", 0), ("col", 1)), 1)
        drop = neighbour_sum(load, weights, drop_ext) / denom
    return drop


def body(demand, leakage, conductance, vias, layer_of, lateral_k, vertical_k):
    tile_rows, tile_cols = demand.shape
    group_layers, cell_rows, therm_cols = lateral_k.shape
    cell_cols = tile_cols // COARSE
    groups = lax.axis_size("col")
    group_index = lax.axis_index("col")
    all_layers = group_layers * groups
    own_ids = lax.dynamic_slice_in_dim(layer_of, group_index * cell_cols, cell_cols, 1)
    coeff_ext = extended(jnp.stack([lateral_k, vertical_k]), (("row", 2), ("col", 1)), 1)
    coeff_ext = jnp.pad(coeff_ext, ((0, 0), (0, 0), (0, 0), (1, 1)))
    lat_ext = coeff_ext[0]
    vert_ext = coeff_ext[1]
    w_north = (lateral_k + lat_ext[1:-1, :-2, 1:-1]) * 0.5
    w_south = (lateral_k + lat_ext[1:-1, 2:, 1:-1]) * 0.5
    w_west = (lateral_k + lat_ext[1:-1, 1:-1, :-2]) * 0.5
    w_east = (lateral_k + lat_ext[1:-1, 1:-1, 2:]) * 0.5
    w_below = (vertical_k + vert_ext[:-2, 1:-1, 1:-1]) * 0.5
    w_above = (vertical_k + vert_ext[2:, 1:-1, 1:-1]) * 0.5
    heat_denom = w_north + w_south + w_west + w_east + w_below + w_above
    drop = jnp.zeros(demand.shape, jnp.float32)
    temp = jnp.zeros(lateral_k.shape, jnp.float32)
    via_g = VIA_CONDUCT * vias.astype(jnp.float32)
    cell_temp = jnp.zeros((cell_rows, cell_cols), jnp.float32)
    for outer in range(OUTER):
        if outer > 0:
            blocks = temp.reshape(group_layers, cell_rows, groups, cell_cols)
            returned = lax.all_to_all(
                blocks, "col", split_axis=2, concat_axis=0, tiled=True
            ).reshape(all_layers, cell_rows, cell_cols)
            layer_ids = jnp.arange(all_layers, dtype=jnp.int32)
            cell_temp = jnp.sum(
                jnp.where(own_ids[None, :, :] == layer_ids[:, None, None], returned, 0.0), axis=0
            )
        fine_temp = fine_of(cell_temp)
        cond = conductance / (1.0 + COND_SLOPE * fine_temp)
        load = demand + leakage * jnp.exp(LEAK_SLOPE * fine_temp)
        drop = power_phase(drop, cond, load, via_g)
        heat = coarse_of(load * (1.0 - drop) + cond * drop * drop)
        layer_grid = jnp.arange(all_layers, dtype=jnp.int32).reshape(groups, group_layers, 1, 1)
        deposit = jnp.where(own_ids[None, None, :, :] == layer_grid, heat[None, None, :, :], 0.0)
        source = lax.all_to_all(deposit, "col", split_axis=0, concat_axis=3, tiled=True).reshape(
            group_layers, cell_rows, therm_cols
        )
        for sweep in range(HEAT_SWEEPS):
            temp_ext = extended(temp, (("row", 1), ("col", 0)), 1)
            temp_ext = jnp.pad(temp_ext, ((0, 0), (0, 0), (1, 1)))
            summed = (
                source
                + w_north * temp_ext[1:-1, :-2, 1:-1]
                + w_south * temp_ext[1:-1, 2:, 1:-1]
                + w_west * temp_ext[1:-1, 1:-1, :-2]
                + w_east * temp_ext[1:-1, 1:-1, 2:]
                + w_below * temp_ext[:-2, 1:-1, 1:-1]
                + w_above * temp_ext[2:, 1:-1, 1:-1]
            )
            temp = summed / heat_denom
    return (drop, temp)


def solution(mesh):
    in_specs = (
        P("row", "col"),
        P("row", "col"),
        P("row", "col"),
        P("row", "col"),
        P("row", None),
        P("col", "row", None),
        P("col", "row", None),
    )
    out_specs = (P("row", "col"), P("col", "row", None))
    return jax.shard_map(body, mesh=mesh, in_specs=in_specs, out_specs=out_specs, check_vma=False)
```

profile of v0, /device:TPU:23, one launch (start us, length us, event | category | flops | bytes accessed | tf_op | source)
XLA Modules:
  0.0 587.0 jit_solution(9496003159957684252)
XLA Ops:
  7.3 6.3 %collective-permute-start.1 = (f32[1,1024]{1,0:T(1,128)S(1)}, f32[1,1024]{1,0:T(1,128)S(1)}, u32[]{:S(2)}, u32[]{:S(2)}) collective-permute-start(f32[1,1024]{1,0:T(1,128)S(1)} %broadcast.98), channel_id=1, source_target_pairs={{0,8},{8,16},{16,24},{24,32},{32,40},{40,48},{48,56},{56,64},{64,7... | collective-permute-start | bytes 12296 | tf_op jit(solution)/shard_map/ppermute | solution.py:22
  22.6 5.5 collective-permute-start.5
  30.2 5.7 collective-permute-done.7
  35.9 4.4 fusion.7
  40.3 7.4 %collective-permute-start.8 = (f32[1,1024]{1,0:T(1,128)S(1)}, f32[1,1024]{1,0:T(1,128)S(1)}, u32[]{:S(2)}, u32[]{:S(2)}) collective-permute-start(f32[1,1024]{1,0:T(1,128)S(1)} %get-tuple-element.87), channel_id=1, source_target_pairs={{0,8},{8,16},{16,24},{24,32},{32,40},{40,48},{48,56},{56,64},{64,7... | collective-permute-start | bytes 12296 | tf_op jit(solution)/shard_map/ppermute | solution.py:22
  49.7 5.4 collective-permute-done.9
  75.1 6.0 %collective-permute-start.24 = (f32[8,1,1024]{2,1,0:T(1,128)}, f32[8,1,1024]{2,1,0:T(1,128)}, u32[]{:S(2)}, u32[]{:S(2)}) collective-permute-start(f32[8,1,1024]{2,1,0:T(1,128)} %broadcast.101), channel_id=1, source_target_pairs={{0,8},{8,16},{16,24},{24,32},{32,40},{40,48},{48,56},{56,64},{64,7... | collective-permute-start | bytes 98312 | tf_op jit(solution)/shard_map/ppermute | solution.py:22
  89.9 6.6 %collective-permute-start.20 = (f32[2,8,1,1024]{3,2,1,0:T(1,128)}, f32[2,8,1,1024]{3,2,1,0:T(1,128)}, u32[]{:S(2)}, u32[]{:S(2)}) collective-permute-start(f32[2,8,1,1024]{3,2,1,0:T(1,128)} %get-tuple-element.21), channel_id=1, source_target_pairs={{0,8},{8,16},{16,24},{24,32},{32,40},{40,48},{48,56},{56,64},{64,7... | collective-permute-start | bytes 196616 | tf_op jit(solution)/shard_map/ppermute | solution.py:22
  96.6 6.2 %fusion.160 = f32[256,1024]{1,0:T(8,128)S(1)} fusion(f32[258,1]{1,0:T(8,128)} %collective-permute-done.15, f32[1,1024]{1,0:T(1,128)} %copy-done.29, f32[256,1024]{1,0:T(8,128)} %copy-done.24, f32[1,1024]{1,0:T(1,128)} %copy-done.28, f32[258,1]{1,0:T(8,128)} %collective-permute-done.14, f32[256,1024]{1,0:T(8,128)} %copy-done.21, ...), kind=kLoop, calls=%fused_computation.345 | loop fusion | flops 10223616 | bytes 5263392 | tf_op jit(solution)/shard_map/div | solution.py:68
  102.8 4.7 collective-permute-start.16
  110.1 4.8 collective-permute-done.17
  124.8 4.6 fusion.18
  129.4 12.1 %reshape.56 = f32[32,8,128,8]{3,2,1,0:T(8,128)} reshape(f32[256,1024]{1,0:T(8,128)} %get-tuple-element.13) | data formatting | bytes 2097152 | tf_op jit(solution)/shard_map/reshape | solution.py:39
  141.5 7.0 %reduce_sum.27 = f32[32,128]{1,0:T(8,128)S(1)} reduce(f32[32,8,128,8]{3,2,1,0:T(8,128)} %reshape.56, f32[]{:T(128)} %constant.8.clone.1), dimensions={1,3}, to_apply=%region_0.1 | reduce | flops 258048 | bytes 1064964 | tf_op jit(solution)/shard_map/reduce_sum | solution.py:39
  157.1 4.2 all-to-all-start
  171.1 10.8 %collective-permute-done.22 = f32[2,1,34,1024]{3,2,1,0:T(8,128)S(1)} collective-permute-done((f32[2,1,34,1024]{3,2,1,0:T(8,128)S(1)}, f32[2,1,34,1024]{3,2,1,0:T(8,128)S(1)}, u32[]{:S(2)}, u32[]{:S(2)}) %collective-permute-start.22) | collective-permute-done | bytes 278560 | tf_op jit(solution)/shard_map/ppermute | solution.py:22
  183.3 4.5 select_maximum_fusion
  192.8 7.7 %fusion.16 = (f32[8,32,1024]{2,1,0:T(8,128)S(1)}, f32[8,32,1024]{2,1,0:T(8,128)S(1)}, f32[8,32,1024]{2,1,0:T(8,128)S(1)}, f32[8,32,1024]{2,1,0:T(8,128)S(1)}, f3...) fusion(f32[8,32,1024]{2,1,0:T(8,128)} %reshape.57, ...), kind=kLoop, calls=%fused_computation.67 | loop fusion | flops 9437184 | bytes 20267008 | tf_op jit(solution)/shard_map/div | solution.py:127
  206.4 5.7 collective-permute-done.29
  218.4 5.6 collective-permute-done.31
  232.6 5.7 collective-permute-done.33
  257.1 5.7 collective-permute-done.37
  277.6 4.2 all-to-all-start.1
  287.9 5.1 all-to-all-done.1
  294.4 8.0 %broadcast_in_dim.48 = f32[32,8,128,8]{3,2,1,0:T(8,128)} broadcast(f32[32,128]{1,0:T(8,128)S(1)} %get-tuple-element.92), dimensions={0,2} | broadcast | bytes 1064960 | tf_op jit(solution)/shard_map/broadcast_in_dim | solution.py:32
  302.4 13.5 %add.440 = f32[256,1024]{1,0:T(8,128)} reshape(f32[32,8,128,8]{3,2,1,0:T(8,128)} %broadcast_in_dim.48) | data formatting | bytes 2097152 | tf_op jit(solution)/shard_map/add | solution.py:106
  324.0 4.8 collective-permute-start.45
  331.6 5.5 collective-permute-start.44
  339.0 8.0 %broadcast_in_dim.47 = f32[32,8,128,8]{3,2,1,0:T(8,128)} broadcast(f32[32,128]{1,0:T(8,128)S(1)} %get-tuple-element.91), dimensions={0,2} | broadcast | bytes 1064960 | tf_op jit(solution)/shard_map/broadcast_in_dim | solution.py:32
  347.0 13.5 %exp.8 = f32[256,1024]{1,0:T(8,128)} reshape(f32[32,8,128,8]{3,2,1,0:T(8,128)} %broadcast_in_dim.47) | data formatting | bytes 2097152 | tf_op jit(solution)/shard_map/exp | solution.py:107
  360.5 8.3 %fusion.93 = (f32[256,1024]{1,0:T(8,128)S(1)}, f32[256,1024]{1,0:T(8,128)S(1)}) fusion(f32[258,1]{1,0:T(8,128)} %collective-permute-done.47, f32[1,1024]{1,0:T(1,128)S(1)} %collective-permute-done.43, f32[256,1024]{1,0:T(8,128)} %get-tuple-element.14, f32[1,1024]{1,0:T(1,128)S(1)} %collective-permute-done.41, f32[258,1]{1,0:T(8,128)} %collective-permute-done.45, ...), kind=kLoop, calls=%fused_computation.210 | loop fusion | flops 10747904 | bytes 8409120 | tf_op jit(solution)/shard_map/div | solution.py:68
  368.9 6.4 %collective-permute-start.48 = (f32[1,1024]{1,0:T(1,128)S(1)}, f32[1,1024]{1,0:T(1,128)S(1)}, u32[]{:S(2)}, u32[]{:S(2)}) collective-permute-start(f32[1,1024]{1,0:T(1,128)S(1)} %get-tuple-element.71), channel_id=1, source_target_pairs={{0,8},{8,16},{16,24},{24,32},{32,40},{40,48},{48,56},{56,64},{64,7... | collective-permute-start | bytes 12296 | tf_op jit(solution)/shard_map/ppermute | solution.py:22
  377.3 5.4 collective-permute-done.49
  382.8 6.4 %collective-permute-start.50 = (f32[258,1]{1,0:T(8,128)S(1)}, f32[258,1]{1,0:T(8,128)S(1)}, u32[]{:S(2)}, u32[]{:S(2)}) collective-permute-start(f32[258,1]{1,0:T(8,128)S(1)} %get-tuple-element.43), channel_id=1, source_target_pairs={{0,1},{1,2},{2,3},{3,4},{4,5},{5,6},{6,7},{8,9},{9,10},{10,11},{11... | collective-permute-start | bytes 3104 | tf_op jit(solution)/shard_map/ppermute | solution.py:22
  391.1 5.9 %collective-permute-done.51 = f32[258,1]{1,0:T(8,128)S(1)} collective-permute-done((f32[258,1]{1,0:T(8,128)S(1)}, f32[258,1]{1,0:T(8,128)S(1)}, u32[]{:S(2)}, u32[]{:S(2)}) %collective-permute-start.51) | collective-permute-done | bytes 1064 | tf_op jit(solution)/shard_map/ppermute | solution.py:25
  406.0 5.4 collective-permute-done.53
  430.0 5.4 collective-permute-done.57
  445.3 4.6 fusion.19
  449.9 12.1 %reshape.59 = f32[32,8,128,8]{3,2,1,0:T(8,128)} reshape(f32[256,1024]{1,0:T(8,128)} %get-tuple-element.2) | data formatting | bytes 2097152 | tf_op jit(solution)/shard_map/reshape | solution.py:39
  461.9 7.0 %reduce_sum.29 = f32[32,128]{1,0:T(8,128)S(1)} reduce(f32[32,8,128,8]{3,2,1,0:T(8,128)} %reshape.59, f32[]{:T(128)} %constant.8.clone.1), dimensions={1,3}, to_apply=%region_2.3 | reduce | flops 258048 | bytes 1064964 | tf_op jit(solution)/shard_map/reduce_sum | solution.py:39
  470.0 4.2 all-to-all-start.2
  480.7 5.7 collective-permute-done.61
  487.5 4.5 collective-permute-start.62
  494.2 5.9 %collective-permute-done.63 = f32[1,34,1024]{2,1,0:T(8,128)S(1)} collective-permute-done((f32[1,34,1024]{2,1,0:T(8,128)S(1)}, f32[1,34,1024]{2,1,0:T(8,128)S(1)}, u32[]{:S(2)}, u32[]{:S(2)}) %collective-permute-start.63) | collective-permute-done | bytes 139296 | tf_op jit(solution)/shard_map/ppermute | solution.py:25
  507.9 5.5 fusion.55
  518.7 5.7 collective-permute-done.65
  543.8 5.7 collective-permute-done.69
  567.3 5.7 collective-permute-done.73
  (258 shorter events, 275.5 us)
Async XLA Ops:
  1.5 14.1 %collective-permute-start = (f32[1,1024]{1,0:T(1,128)S(1)}, f32[1,1024]{1,0:T(1,128)S(1)}, u32[]{:S(2)}, u32[]{:S(2)}) collective-permute-start(f32[1,1024]{1,0:T(1,128)S(1)} %get-tuple-element.90), channel_id=1, source_target_pairs={{0,8},{8,16},{16,24},{24,32},{32,40},{40,48},{48,56},{56,64},{64,7... | collective-permute-start | bytes 12296 | tf_op jit(solution)/shard_map/ppermute | solution.py:22
  5.3 10.2 %collective-permute-start.2 = (f32[1,1024]{1,0:T(1,128)S(1)}, f32[1,1024]{1,0:T(1,128)S(1)}, u32[]{:S(2)}, u32[]{:S(2)}) collective-permute-start(f32[1,1024]{1,0:T(1,128)S(1)} %get-tuple-element.89), channel_id=1, source_target_pairs={{8,0},{16,8},{24,16},{32,24},{40,32},{48,40},{56,48},{64,56},{72,6... | collective-permute-start | bytes 12296 | tf_op jit(solution)/shard_map/ppermute | solution.py:25
  7.3 15.0 %collective-permute-start.1 = (f32[1,1024]{1,0:T(1,128)S(1)}, f32[1,1024]{1,0:T(1,128)S(1)}, u32[]{:S(2)}, u32[]{:S(2)}) collective-permute-start(f32[1,1024]{1,0:T(1,128)S(1)} %broadcast.98), channel_id=1, source_target_pairs={{0,8},{8,16},{16,24},{24,32},{32,40},{40,48},{48,56},{56,64},{64,7... | collective-permute-start | bytes 12296 | tf_op jit(solution)/shard_map/ppermute | solution.py:22
  13.6 8.7 %collective-permute-start.3 = (f32[1,1024]{1,0:T(1,128)S(1)}, f32[1,1024]{1,0:T(1,128)S(1)}, u32[]{:S(2)}, u32[]{:S(2)}) collective-permute-start(f32[1,1024]{1,0:T(1,128)S(1)} %broadcast.98), channel_id=1, source_target_pairs={{8,0},{16,8},{24,16},{32,24},{40,32},{48,40},{56,48},{64,56},{72,6... | collective-permute-start | bytes 12296 | tf_op jit(solution)/shard_map/ppermute | solution.py:25
  16.7 13.3 %collective-permute-start.4 = (f32[258,1]{1,0:T(8,128)S(1)}, f32[258,1]{1,0:T(8,128)S(1)}, u32[]{:S(2)}, u32[]{:S(2)}) collective-permute-start(f32[258,1]{1,0:T(8,128)S(1)} %get-tuple-element.56), channel_id=1, source_target_pairs={{0,1},{1,2},{2,3},{3,4},{4,5},{5,6},{6,7},{8,9},{9,10},{10,11},{11... | collective-permute-start | bytes 3104 | tf_op jit(solution)/shard_map/ppermute | solution.py:22
  20.4 9.6 %collective-permute-start.6 = (f32[258,1]{1,0:T(8,128)S(1)}, f32[258,1]{1,0:T(8,128)S(1)}, u32[]{:S(2)}, u32[]{:S(2)}) collective-permute-start(f32[258,1]{1,0:T(8,128)S(1)} %get-tuple-element.55), channel_id=1, source_target_pairs={{1,0},{2,1},{3,2},{4,3},{5,4},{6,5},{7,6},{9,8},{10,9},{11,10},{12... | collective-permute-start | bytes 3104 | tf_op jit(solution)/shard_map/ppermute | solution.py:25
  22.6 7.7 %collective-permute-start.5 = (f32[258,1]{1,0:T(8,128)S(1)}, f32[258,1]{1,0:T(8,128)S(1)}, u32[]{:S(2)}, u32[]{:S(2)}) collective-permute-start(f32[258,1]{1,0:T(8,128)S(1)} %get-tuple-element.57), channel_id=1, source_target_pairs={{0,1},{1,2},{2,3},{3,4},{4,5},{5,6},{6,7},{8,9},{9,10},{10,11},{11... | collective-permute-start | bytes 3104 | tf_op jit(solution)/shard_map/ppermute | solution.py:22
  28.1 7.9 %collective-permute-start.7 = (f32[258,1]{1,0:T(8,128)S(1)}, f32[258,1]{1,0:T(8,128)S(1)}, u32[]{:S(2)}, u32[]{:S(2)}) collective-permute-start(f32[258,1]{1,0:T(8,128)S(1)} %get-tuple-element.58), channel_id=1, source_target_pairs={{1,0},{2,1},{3,2},{4,3},{5,4},{6,5},{7,6},{9,8},{10,9},{11,10},{12... | collective-permute-start | bytes 3104 | tf_op jit(solution)/shard_map/ppermute | solution.py:25
  40.3 9.4 %collective-permute-start.8 = (f32[1,1024]{1,0:T(1,128)S(1)}, f32[1,1024]{1,0:T(1,128)S(1)}, u32[]{:S(2)}, u32[]{:S(2)}) collective-permute-start(f32[1,1024]{1,0:T(1,128)S(1)} %get-tuple-element.87), channel_id=1, source_target_pairs={{0,8},{8,16},{16,24},{24,32},{32,40},{40,48},{48,56},{56,64},{64,7... | collective-permute-start | bytes 12296 | tf_op jit(solution)/shard_map/ppermute | solution.py:22
  57.1 7.9 %collective-permute-start.11 = (f32[258,1]{1,0:T(8,128)S(1)}, f32[258,1]{1,0:T(8,128)S(1)}, u32[]{:S(2)}, u32[]{:S(2)}) collective-permute-start(f32[258,1]{1,0:T(8,128)S(1)} %get-tuple-element.54), channel_id=1, source_target_pairs={{1,0},{2,1},{3,2},{4,3},{5,4},{6,5},{7,6},{9,8},{10,9},{11,10},{12... | collective-permute-start | bytes 3104 | tf_op jit(solution)/shard_map/ppermute | solution.py:25
  68.5 14.6 %collective-permute-start.12 = (f32[1,1024]{1,0:T(1,128)S(1)}, f32[1,1024]{1,0:T(1,128)S(1)}, u32[]{:S(2)}, u32[]{:S(2)}) collective-permute-start(f32[1,1024]{1,0:T(1,128)S(1)} %get-tuple-element.85), channel_id=1, source_target_pairs={{0,8},{8,16},{16,24},{24,32},{32,40},{40,48},{48,56},{56,64},{64,7... | collective-permute-start | bytes 12296 | tf_op jit(solution)/shard_map/ppermute | solution.py:22
  72.5 10.5 %collective-permute-start.13 = (f32[1,1024]{1,0:T(1,128)S(1)}, f32[1,1024]{1,0:T(1,128)S(1)}, u32[]{:S(2)}, u32[]{:S(2)}) collective-permute-start(f32[1,1024]{1,0:T(1,128)S(1)} %get-tuple-element.86), channel_id=1, source_target_pairs={{8,0},{16,8},{24,16},{32,24},{40,32},{48,40},{56,48},{64,56},{72,6... | collective-permute-start | bytes 12296 | tf_op jit(solution)/shard_map/ppermute | solution.py:25
  75.1 73.4 %collective-permute-start.24 = (f32[8,1,1024]{2,1,0:T(1,128)}, f32[8,1,1024]{2,1,0:T(1,128)}, u32[]{:S(2)}, u32[]{:S(2)}) collective-permute-start(f32[8,1,1024]{2,1,0:T(1,128)} %broadcast.101), channel_id=1, source_target_pairs={{0,8},{8,16},{16,24},{24,32},{32,40},{40,48},{48,56},{56,64},{64,7... | collective-permute-start | bytes 98312 | tf_op jit(solution)/shard_map/ppermute | solution.py:22
  81.1 67.3 %collective-permute-start.25 = (f32[8,1,1024]{2,1,0:T(1,128)}, f32[8,1,1024]{2,1,0:T(1,128)}, u32[]{:S(2)}, u32[]{:S(2)}) collective-permute-start(f32[8,1,1024]{2,1,0:T(1,128)} %broadcast.101), channel_id=1, source_target_pairs={{8,0},{16,8},{24,16},{32,24},{40,32},{48,40},{56,48},{64,56},{72,6... | collective-permute-start | bytes 98312 | tf_op jit(solution)/shard_map/ppermute | solution.py:25
  83.8 12.7 %collective-permute-start.14 = (f32[258,1]{1,0:T(8,128)}, f32[258,1]{1,0:T(8,128)}, u32[]{:S(2)}, u32[]{:S(2)}) collective-permute-start(f32[258,1]{1,0:T(8,128)} %get-tuple-element.51), channel_id=1, source_target_pairs={{0,1},{1,2},{2,3},{3,4},{4,5},{5,6},{6,7},{8,9},{9,10},{10,11},{11... | collective-permute-start | bytes 3104 | tf_op jit(solution)/shard_map/ppermute | solution.py:22
  85.8 10.8 %collective-permute-start.15 = (f32[258,1]{1,0:T(8,128)}, f32[258,1]{1,0:T(8,128)}, u32[]{:S(2)}, u32[]{:S(2)}) collective-permute-start(f32[258,1]{1,0:T(8,128)} %get-tuple-element.52), channel_id=1, source_target_pairs={{1,0},{2,1},{3,2},{4,3},{5,4},{6,5},{7,6},{9,8},{10,9},{11,10},{12... | collective-permute-start | bytes 3104 | tf_op jit(solution)/shard_map/ppermute | solution.py:25
  89.9 71.3 %collective-permute-start.20 = (f32[2,8,1,1024]{3,2,1,0:T(1,128)}, f32[2,8,1,1024]{3,2,1,0:T(1,128)}, u32[]{:S(2)}, u32[]{:S(2)}) collective-permute-start(f32[2,8,1,1024]{3,2,1,0:T(1,128)} %get-tuple-element.21), channel_id=1, source_target_pairs={{0,8},{8,16},{16,24},{24,32},{32,40},{40,48},{48,56},{56,64},{64,7... | collective-permute-start | bytes 196616 | tf_op jit(solution)/shard_map/ppermute | solution.py:22
  116.9 7.9 %collective-permute-start.19 = (f32[258,1]{1,0:T(8,128)S(1)}, f32[258,1]{1,0:T(8,128)S(1)}, u32[]{:S(2)}, u32[]{:S(2)}) collective-permute-start(f32[258,1]{1,0:T(8,128)S(1)} %get-tuple-element.50), channel_id=1, source_target_pairs={{1,0},{2,1},{3,2},{4,3},{5,4},{6,5},{7,6},{9,8},{10,9},{11,10},{12... | collective-permute-start | bytes 3104 | tf_op jit(solution)/shard_map/ppermute | solution.py:25
  121.0 40.3 %collective-permute-start.21 = (f32[2,8,1,1024]{3,2,1,0:T(1,128)}, f32[2,8,1,1024]{3,2,1,0:T(1,128)S(1)}, u32[]{:S(2)}, u32[]{:S(2)}) collective-permute-start(f32[2,8,1,1024]{3,2,1,0:T(1,128)} %get-tuple-element.22), channel_id=1, source_target_pairs={{8,0},{16,8},{24,16},{32,24},{40,32},{48,40},{56,48},{64,56},{72,6... | collective-permute-start | bytes 196616 | tf_op jit(solution)/shard_map/ppermute | solution.py:25
  150.1 18.1 %collective-permute-start.26 = (f32[1,34,1024]{2,1,0:T(8,128)}, f32[1,34,1024]{2,1,0:T(8,128)S(1)}, u32[]{:S(2)}, u32[]{:S(2)}) collective-permute-start(f32[1,34,1024]{2,1,0:T(8,128)} %get-tuple-element.37), channel_id=1, source_target_pairs={{0,1},{1,2},{2,3},{3,4},{4,5},{5,6},{6,7},{8,9},{9,10},{10,11},{11... | collective-permute-start | bytes 417800 | tf_op jit(solution)/shard_map/ppermute | solution.py:22
  152.2 16.0 %collective-permute-start.27 = (f32[1,34,1024]{2,1,0:T(8,128)}, f32[1,34,1024]{2,1,0:T(8,128)}, u32[]{:S(2)}, u32[]{:S(2)}) collective-permute-start(f32[1,34,1024]{2,1,0:T(8,128)} %get-tuple-element.38), channel_id=1, source_target_pairs={{1,0},{2,1},{3,2},{4,3},{5,4},{6,5},{7,6},{9,8},{10,9},{11,10},{12... | collective-permute-start | bytes 417800 | tf_op jit(solution)/shard_map/ppermute | solution.py:25
  157.1 32.7 %all-to-all-start = ((f32[8,8,32,128]{3,2,1,0:T(8,128)}), f32[8,8,32,128]{3,2,1,0:T(8,128)}, u32[]{:S(2)}, u32[]{:S(2)}) async-start(f32[8,8,32,128]{3,2,1,0:T(8,128)} %compare_select_fusion.1), calls=%async_computation | async-start | bytes 2097152 | tf_op jit(solution)/shard_map/all_to_all | solution.py:112
  162.1 19.8 %collective-permute-start.22 = (f32[2,1,34,1024]{3,2,1,0:T(8,128)S(1)}, f32[2,1,34,1024]{3,2,1,0:T(8,128)S(1)}, u32[]{:S(2)}, u32[]{:S(2)}) collective-permute-start(f32[2,1,34,1024]{3,2,1,0:T(8,128)S(1)} %get-tuple-element.19), channel_id=1, source_target_pairs={{0,1},{1,2},{2,3},{3,4},{4,5},{5,6},{6,7},{8,9},{9,10},{10,11},{11... | collective-permute-start | bytes 835592 | tf_op jit(solution)/shard_map/ppermute | solution.py:22
  166.3 17.0 %collective-permute-start.23 = (f32[2,1,34,1024]{3,2,1,0:T(8,128)S(1)}, f32[2,1,34,1024]{3,2,1,0:T(8,128)S(1)}, u32[]{:S(2)}, u32[]{:S(2)}) collective-permute-start(f32[2,1,34,1024]{3,2,1,0:T(8,128)S(1)} %get-tuple-element.20), channel_id=1, source_target_pairs={{1,0},{2,1},{3,2},{4,3},{5,4},{6,5},{7,6},{9,8},{10,9},{11,10},{12... | collective-permute-start | bytes 835592 | tf_op jit(solution)/shard_map/ppermute | solution.py:25
  204.5 7.6 %collective-permute-start.29 = (f32[8,1,1024]{2,1,0:T(1,128)S(1)}, f32[8,1,1024]{2,1,0:T(1,128)S(1)}, u32[]{:S(2)}, u32[]{:S(2)}) collective-permute-start(f32[8,1,1024]{2,1,0:T(1,128)S(1)} %get-tuple-element.82), channel_id=1, source_target_pairs={{8,0},{16,8},{24,16},{32,24},{40,32},{48,40},{56,48},{64,56},{72,6... | collective-permute-start | bytes 98312 | tf_op jit(solution)/shard_map/ppermute | solution.py:25
  215.8 8.2 %collective-permute-start.31 = (f32[1,34,1024]{2,1,0:T(8,128)S(1)}, f32[1,34,1024]{2,1,0:T(8,128)S(1)}, u32[]{:S(2)}, u32[]{:S(2)}) collective-permute-start(f32[1,34,1024]{2,1,0:T(8,128)S(1)} %get-tuple-element.36), channel_id=1, source_target_pairs={{1,0},{2,1},{3,2},{4,3},{5,4},{6,5},{7,6},{9,8},{10,9},{11,10},{12... | collective-permute-start | bytes 417800 | tf_op jit(solution)/shard_map/ppermute | solution.py:25
  230.6 7.6 %collective-permute-start.33 = (f32[8,1,1024]{2,1,0:T(1,128)S(1)}, f32[8,1,1024]{2,1,0:T(1,128)S(1)}, u32[]{:S(2)}, u32[]{:S(2)}) collective-permute-start(f32[8,1,1024]{2,1,0:T(1,128)S(1)} %get-tuple-element.80), channel_id=1, source_target_pairs={{8,0},{16,8},{24,16},{32,24},{40,32},{48,40},{56,48},{64,56},{72,6... | collective-permute-start | bytes 98312 | tf_op jit(solution)/shard_map/ppermute | solution.py:25
  240.2 8.2 %collective-permute-start.35 = (f32[1,34,1024]{2,1,0:T(8,128)S(1)}, f32[1,34,1024]{2,1,0:T(8,128)S(1)}, u32[]{:S(2)}, u32[]{:S(2)}) collective-permute-start(f32[1,34,1024]{2,1,0:T(8,128)S(1)} %get-tuple-element.34), channel_id=1, source_target_pairs={{1,0},{2,1},{3,2},{4,3},{5,4},{6,5},{7,6},{9,8},{10,9},{11,10},{12... | collective-permute-start | bytes 417800 | tf_op jit(solution)/shard_map/ppermute | solution.py:25
  264.8 8.2 %collective-permute-start.39 = (f32[1,34,1024]{2,1,0:T(8,128)S(1)}, f32[1,34,1024]{2,1,0:T(8,128)S(1)}, u32[]{:S(2)}, u32[]{:S(2)}) collective-permute-start(f32[1,34,1024]{2,1,0:T(8,128)S(1)} %get-tuple-element.32), channel_id=1, source_target_pairs={{1,0},{2,1},{3,2},{4,3},{5,4},{6,5},{7,6},{9,8},{10,9},{11,10},{12... | collective-permute-start | bytes 417800 | tf_op jit(solution)/shard_map/ppermute | solution.py:25
  277.6 15.4 %all-to-all-start.1 = ((f32[8,32,8,128]{3,1,0,2:T(8,128)}), f32[8,32,8,128]{3,1,0,2:T(8,128)}, u32[]{:S(2)}, u32[]{:S(2)}) async-start(f32[8,32,8,128]{3,1,0,2:T(8,128)} %copy_bitcast_fusion), calls=%async_computation.1 | async-start | bytes 2097152 | tf_op jit(solution)/shard_map/all_to_all | solution.py:98
  282.6 40.6 %collective-permute-start.41 = (f32[1,1024]{1,0:T(1,128)S(1)}, f32[1,1024]{1,0:T(1,128)S(1)}, u32[]{:S(2)}, u32[]{:S(2)}) collective-permute-start(f32[1,1024]{1,0:T(1,128)S(1)} %get-tuple-element.75), channel_id=1, source_target_pairs={{0,8},{8,16},{16,24},{24,32},{32,40},{40,48},{48,56},{56,64},{64,7... | collective-permute-start | bytes 12296 | tf_op jit(solution)/shard_map/ppermute | solution.py:22
  286.0 37.3 %collective-permute-start.43 = (f32[1,1024]{1,0:T(1,128)S(1)}, f32[1,1024]{1,0:T(1,128)S(1)}, u32[]{:S(2)}, u32[]{:S(2)}) collective-permute-start(f32[1,1024]{1,0:T(1,128)S(1)} %get-tuple-element.76), channel_id=1, source_target_pairs={{8,0},{16,8},{24,16},{32,24},{40,32},{48,40},{56,48},{64,56},{72,6... | collective-permute-start | bytes 12296 | tf_op jit(solution)/shard_map/ppermute | solution.py:25
  317.7 13.0 %collective-permute-start.40 = (f32[1,1024]{1,0:T(1,128)S(1)}, f32[1,1024]{1,0:T(1,128)S(1)}, u32[]{:S(2)}, u32[]{:S(2)}) collective-permute-start(f32[1,1024]{1,0:T(1,128)S(1)} %get-tuple-element.74), channel_id=1, source_target_pairs={{0,8},{8,16},{16,24},{24,32},{32,40},{40,48},{48,56},{56,64},{64,7... | collective-permute-start | bytes 12296 | tf_op jit(solution)/shard_map/ppermute | solution.py:22
  321.3 9.5 %collective-permute-start.42 = (f32[1,1024]{1,0:T(1,128)S(1)}, f32[1,1024]{1,0:T(1,128)S(1)}, u32[]{:S(2)}, u32[]{:S(2)}) collective-permute-start(f32[1,1024]{1,0:T(1,128)S(1)} %get-tuple-element.73), channel_id=1, source_target_pairs={{8,0},{16,8},{24,16},{32,24},{40,32},{48,40},{56,48},{64,56},{72,6... | collective-permute-start | bytes 12296 | tf_op jit(solution)/shard_map/ppermute | solution.py:25
  324.0 36.4 %collective-permute-start.45 = (f32[258,1]{1,0:T(8,128)}, f32[258,1]{1,0:T(8,128)}, u32[]{:S(2)}, u32[]{:S(2)}) collective-permute-start(f32[258,1]{1,0:T(8,128)} %get-tuple-element.47), channel_id=1, source_target_pairs={{0,1},{1,2},{2,3},{3,4},{4,5},{5,6},{6,7},{8,9},{9,10},{10,11},{11... | collective-permute-start | bytes 3104 | tf_op jit(solution)/shard_map/ppermute | solution.py:22
  328.8 31.7 %collective-permute-start.47 = (f32[258,1]{1,0:T(8,128)}, f32[258,1]{1,0:T(8,128)}, u32[]{:S(2)}, u32[]{:S(2)}) collective-permute-start(f32[258,1]{1,0:T(8,128)} %get-tuple-element.48), channel_id=1, source_target_pairs={{1,0},{2,1},{3,2},{4,3},{5,4},{6,5},{7,6},{9,8},{10,9},{11,10},{12... | collective-permute-start | bytes 3104 | tf_op jit(solution)/shard_map/ppermute | solution.py:25
  331.6 28.9 %collective-permute-start.44 = (f32[258,1]{1,0:T(8,128)}, f32[258,1]{1,0:T(8,128)S(1)}, u32[]{:S(2)}, u32[]{:S(2)}) collective-permute-start(f32[258,1]{1,0:T(8,128)} %get-tuple-element.46), channel_id=1, source_target_pairs={{0,1},{1,2},{2,3},{3,4},{4,5},{5,6},{6,7},{8,9},{9,10},{10,11},{11... | collective-permute-start | bytes 3104 | tf_op jit(solution)/shard_map/ppermute | solution.py:22
  337.1 23.4 %collective-permute-start.46 = (f32[258,1]{1,0:T(8,128)}, f32[258,1]{1,0:T(8,128)S(1)}, u32[]{:S(2)}, u32[]{:S(2)}) collective-permute-start(f32[258,1]{1,0:T(8,128)} %get-tuple-element.45), channel_id=1, source_target_pairs={{1,0},{2,1},{3,2},{4,3},{5,4},{6,5},{7,6},{9,8},{10,9},{11,10},{12... | collective-permute-start | bytes 3104 | tf_op jit(solution)/shard_map/ppermute | solution.py:25
  368.9 8.4 %collective-permute-start.48 = (f32[1,1024]{1,0:T(1,128)S(1)}, f32[1,1024]{1,0:T(1,128)S(1)}, u32[]{:S(2)}, u32[]{:S(2)}) collective-permute-start(f32[1,1024]{1,0:T(1,128)S(1)} %get-tuple-element.71), channel_id=1, source_target_pairs={{0,8},{8,16},{16,24},{24,32},{32,40},{40,48},{48,56},{56,64},{64,7... | collective-permute-start | bytes 12296 | tf_op jit(solution)/shard_map/ppermute | solution.py:22
  382.8 8.3 %collective-permute-start.50 = (f32[258,1]{1,0:T(8,128)S(1)}, f32[258,1]{1,0:T(8,128)S(1)}, u32[]{:S(2)}, u32[]{:S(2)}) collective-permute-start(f32[258,1]{1,0:T(8,128)S(1)} %get-tuple-element.43), channel_id=1, source_target_pairs={{0,1},{1,2},{2,3},{3,4},{4,5},{5,6},{6,7},{8,9},{9,10},{10,11},{11... | collective-permute-start | bytes 3104 | tf_op jit(solution)/shard_map/ppermute | solution.py:22
  389.1 7.9 %collective-permute-start.51 = (f32[258,1]{1,0:T(8,128)S(1)}, f32[258,1]{1,0:T(8,128)S(1)}, u32[]{:S(2)}, u32[]{:S(2)}) collective-permute-start(f32[258,1]{1,0:T(8,128)S(1)} %get-tuple-element.44), channel_id=1, source_target_pairs={{1,0},{2,1},{3,2},{4,3},{5,4},{6,5},{7,6},{9,8},{10,9},{11,10},{12... | collective-permute-start | bytes 3104 | tf_op jit(solution)/shard_map/ppermute | solution.py:25
  413.7 7.9 %collective-permute-start.55 = (f32[258,1]{1,0:T(8,128)S(1)}, f32[258,1]{1,0:T(8,128)S(1)}, u32[]{:S(2)}, u32[]{:S(2)}) collective-permute-start(f32[258,1]{1,0:T(8,128)S(1)} %get-tuple-element.42), channel_id=1, source_target_pairs={{1,0},{2,1},{3,2},{4,3},{5,4},{6,5},{7,6},{9,8},{10,9},{11,10},{12... | collective-permute-start | bytes 3104 | tf_op jit(solution)/shard_map/ppermute | solution.py:25
  437.4 7.9 %collective-permute-start.59 = (f32[258,1]{1,0:T(8,128)S(1)}, f32[258,1]{1,0:T(8,128)S(1)}, u32[]{:S(2)}, u32[]{:S(2)}) collective-permute-start(f32[258,1]{1,0:T(8,128)S(1)} %get-tuple-element.40), channel_id=1, source_target_pairs={{1,0},{2,1},{3,2},{4,3},{5,4},{6,5},{7,6},{9,8},{10,9},{11,10},{12... | collective-permute-start | bytes 3104 | tf_op jit(solution)/shard_map/ppermute | solution.py:25
  470.0 32.7 %all-to-all-start.2 = ((f32[8,8,32,128]{3,2,1,0:T(8,128)}), f32[8,8,32,128]{3,2,1,0:T(8,128)}, u32[]{:S(2)}, u32[]{:S(2)}) async-start(f32[8,8,32,128]{3,2,1,0:T(8,128)} %compare_select_fusion), calls=%async_computation.2 | async-start | bytes 2097152 | tf_op jit(solution)/shard_map/all_to_all | solution.py:112
  492.0 8.2 %collective-permute-start.63 = (f32[1,34,1024]{2,1,0:T(8,128)S(1)}, f32[1,34,1024]{2,1,0:T(8,128)S(1)}, u32[]{:S(2)}, u32[]{:S(2)}) collective-permute-start(f32[1,34,1024]{2,1,0:T(8,128)S(1)} %get-tuple-element.30), channel_id=1, source_target_pairs={{1,0},{2,1},{3,2},{4,3},{5,4},{6,5},{7,6},{9,8},{10,9},{11,10},{12... | collective-permute-start | bytes 417800 | tf_op jit(solution)/shard_map/ppermute | solution.py:25
  527.1 8.2 %collective-permute-start.67 = (f32[1,34,1024]{2,1,0:T(8,128)S(1)}, f32[1,34,1024]{2,1,0:T(8,128)S(1)}, u32[]{:S(2)}, u32[]{:S(2)}) collective-permute-start(f32[1,34,1024]{2,1,0:T(8,128)S(1)} %get-tuple-element.28), channel_id=1, source_target_pairs={{1,0},{2,1},{3,2},{4,3},{5,4},{6,5},{7,6},{9,8},{10,9},{11,10},{12... | collective-permute-start | bytes 417800 | tf_op jit(solution)/shard_map/ppermute | solution.py:25
  551.5 8.2 %collective-permute-start.71 = (f32[1,34,1024]{2,1,0:T(8,128)S(1)}, f32[1,34,1024]{2,1,0:T(8,128)S(1)}, u32[]{:S(2)}, u32[]{:S(2)}) collective-permute-start(f32[1,34,1024]{2,1,0:T(8,128)S(1)} %get-tuple-element.26), channel_id=1, source_target_pairs={{1,0},{2,1},{3,2},{4,3},{5,4},{6,5},{7,6},{9,8},{10,9},{11,10},{12... | collective-permute-start | bytes 417800 | tf_op jit(solution)/shard_map/ppermute | solution.py:25
  575.0 8.2 %collective-permute-start.75 = (f32[1,34,1024]{2,1,0:T(8,128)S(1)}, f32[1,34,1024]{2,1,0:T(8,128)S(1)}, u32[]{:S(2)}, u32[]{:S(2)}) collective-permute-start(f32[1,34,1024]{2,1,0:T(8,128)S(1)} %get-tuple-element.24), channel_id=1, source_target_pairs={{1,0},{2,1},{3,2},{4,3},{5,4},{6,5},{7,6},{9,8},{10,9},{11,10},{12... | collective-permute-start | bytes 417800 | tf_op jit(solution)/shard_map/ppermute | solution.py:25
  (61 other events, 965.6 us)
where the time goes:
time: 599 us; the launch traced here: 587 us
  starting transfers between devices  247 us (41%)
  waiting for transfers between devices  148 us (25%)
  other arithmetic  104 us (17%)
  local copies, waits for them, and re-layouts  84.8 us (14%)
    ppermute x38, starting transfers between devices, extended(): lax.ppermute(lax.slice_in_dim(block, block.shape[dim] - width, None, axis...  145 us
    ppermute x38, waiting for transfers between devices, extended(): lax.ppermute(lax.slice_in_dim(block, 0, width, axis=dim), axis, backward)  123 us
    ppermute x38, starting transfers between devices, extended(): lax.ppermute(lax.slice_in_dim(block, 0, width, axis=dim), axis, backward)  89.2 us
    div x6, other arithmetic, power_phase(): drop = neighbour_sum(load, weights, drop_ext) / denom  29.1 us
    div x8, other arithmetic, body(): temp = summed / heat_denom  24.9 us
    reshape x2, local copies, waits for them, and re-layouts, coarse_of(): fine.reshape(count_rows, COARSE, count_cols, COARSE)  24.1 us
    ppermute x38, waiting for transfers between devices, extended(): lax.ppermute(lax.slice_in_dim(block, block.shape[dim] - width, None, axis...  19.9 us
    broadcast_in_dim x2, local copies, waits for them, and re-layouts, fine_of(): jnp.broadcast_to(coarse[:, None, :, None], (count_rows, COARSE, count_col...  16.1 us
  transfers between devices with their start and end apart: 79, of which 40 were waited for; matrix products, arithmetic and copies ran while one was open for 17% of the time, Pallas kernels for 0%

commit v1 on v0

v1 whole, which is shorter than its diff:
```python
import functools

import jax
import jax.numpy as jnp
from jax import lax
from jax.experimental import pallas as pl
from jax.experimental.pallas import tpu as pltpu
from jax.sharding import PartitionSpec as P

COARSE = 8
SWEEPS = 4
HEAT_SWEEPS = 4
COND_SLOPE = 0.5
LEAK_SLOPE = 0.7
VIA_CONDUCT = 4.0

MESH = pl.DeviceIdType.MESH
HIGH = lax.Precision.HIGHEST
F32 = jnp.float32
LINKS = 128


def reciprocal(value):
    return 1.0 / value


def pooled(left, right):
    return jnp.dot(left, right, precision=HIGH, preferred_element_type=F32)


def kernel(
    sizes,
    demand,
    leakage,
    conductance,
    vias,
    layer_of,
    lateral,
    vertical,
    drop_out,
    temp_out,
    p_cond,
    p_dem,
    p_leak,
    p_via,
    c_now,
    load,
    a_n,
    a_s,
    a_w,
    a_e,
    b_p,
    d_0,
    d_1,
    stage,
    stage_i,
    pl_send,
    pr_send,
    pl_recv,
    pr_recv,
    layers,
    lat,
    ver,
    t_n,
    t_s,
    t_w,
    t_e,
    t_b,
    t_a,
    t_r,
    b_t,
    r_far,
    temp_0,
    temp_1,
    pool,
    spread,
    rows_sum,
    heat_own,
    heat_all,
    part,
    part_recv,
    cell,
    g_up,
    e_up,
    load_sem,
    out_sem,
    send_sem,
    recv_sem,
):
    NR, NC, TR, GL, CR = sizes
    NT = 8
    TQ = TR // 4
    row = lax.axis_index("row")
    col = lax.axis_index("col")
    up, down = lax.rem(row + NR - 1, NR), lax.rem(row + 1, NR)
    left, right = lax.rem(col + NC - 1, NC), lax.rem(col + 1, NC)
    peers = [lax.rem(col + k, NC) for k in range(1, NC)]
    count = [0]

    def send(src, dst, device):
        slot = count[0]
        count[0] += 1
        copy = pltpu.make_async_remote_copy(
            src_ref=src,
            dst_ref=dst,
            send_sem=send_sem.at[slot],
            recv_sem=recv_sem.at[slot],
            device_id=device,
            device_id_type=MESH,
        )
        copy.start()
        return copy

    lane = lax.broadcasted_iota(jnp.int32, (8, 128), 1)
    sub = lax.broadcasted_iota(jnp.int32, (8, 128), 0)
    first_lane = lane == 0
    last_lane = lane == 127

    def west_east(tiles):
        n = len(tiles)
        plus = [pltpu.roll(x, 1, axis=1) for x in tiles]
        minus = [pltpu.roll(x, 127, axis=1) for x in tiles]
        west = [jnp.where(first_lane, plus[t - 1], plus[t]) for t in range(n)]
        east = [jnp.where(last_lane, minus[(t + 1) % n], minus[t]) for t in range(n)]
        return west, east

    power = ((conductance, p_cond), (demand, p_dem), (leakage, p_leak), (vias, p_via))
    for index, (src, dst) in enumerate(power):
        for t in range(NT):
            pltpu.make_async_copy(
                src.at[:, pl.ds(128 * t, 128)], dst.at[t, pl.ds(16, TR), :], load_sem.at[index]
            ).start()
    for t in range(NC):
        cut = pl.ds(128 * t, 128)
        pltpu.make_async_copy(
            lateral.at[:, :, cut], lat.at[:, t, pl.ds(8, CR), :], load_sem.at[4]
        ).start()
        pltpu.make_async_copy(
            vertical.at[:, :, cut], ver.at[pl.ds(1, GL), t], load_sem.at[5]
        ).start()
        pltpu.make_async_copy(layer_of.at[:, cut], layers.at[t], load_sem.at[6]).start()

    def loaded(index, ref):
        pltpu.make_async_copy(ref, ref, load_sem.at[index]).wait()

    barrier = pltpu.get_barrier_semaphore()
    near = [(row, p) for p in peers]
    near += [(r, c) for r in (up, down) for c in (col, left, right)]
    for device in near:
        pl.semaphore_signal(barrier, inc=1, device_id=device, device_id_type=MESH)
    pl.semaphore_wait(barrier, len(near))

    row_copies = []
    for index, src in enumerate((conductance, demand, leakage, vias)):
        for side, start, device in ((0, TR - 8, (down, col)), (1, 0, (up, col))):
            dst = stage_i.at[side] if index == 3 else stage.at[side, index]
            row_copies.append(send(src.at[pl.ds(start, 8), :], dst, device))
    ver_copies = []

    def pool_body(i, carry):
        r = lax.broadcasted_iota(jnp.int32, (128, 128), 0)
        c = lax.broadcasted_iota(jnp.int32, (128, 128), 1)
        start = pl.multiple_of(i * 128, 128)
        pool[pl.ds(start, 128), :] = jnp.where(16 * i + r // 8 == c, 1.0 / 64.0, 0.0)
        spread[i] = jnp.where(16 * i + c // 8 == r, 1.0, 0.0)
        return carry

    lax.fori_loop(0, NT, pool_body, 0)

    for index, (_, dst) in enumerate(power):
        loaded(index, dst.at[pl.ds(0, NT), pl.ds(16, TR), :])

    def pack_body(i, carry):
        base = pl.multiple_of(8 * i, 8)
        acc_l = acc_r = jnp.zeros((8, 128), F32)
        for q in range(4):
            for a, ref in enumerate((p_cond, p_dem, p_leak, p_via)):
                at = 32 * q + 8 * a
                rows = pl.ds(16 + q * TQ + base, 8)
                lo = ref[0, rows, :].astype(F32)
                hi = ref[NT - 1, rows, :].astype(F32)
                here = lane // 8 == at // 8
                acc_l = jnp.where(here, pltpu.roll(lo, at, axis=1), acc_l)
                acc_r = jnp.where(here, pltpu.roll(hi, (at + 8) % 128, axis=1), acc_r)
        pl_send[pl.ds(base, 8), :] = acc_l
        pr_send[pl.ds(base, 8), :] = acc_r
        return carry

    lax.fori_loop(0, TQ // 8, pack_body, 0)
    col_copies = []
    for src, dst, c in ((pl_send, pl_recv, left), (pr_send, pr_recv, right)):
        col_copies.append(send(src, dst.at[pl.ds(8, TQ), :], (row, c)))
        col_copies.append(send(src.at[pl.ds(TQ - 8, 8), :], dst.at[pl.ds(0, 8), :], (down, c)))
        col_copies.append(send(src.at[pl.ds(0, 8), :], dst.at[pl.ds(TQ + 8, 8), :], (up, c)))

    for t in range(NC):
        cut = pl.ds(128 * t, 128)
        ver_copies.append(send(vertical.at[GL - 1, :, cut], ver.at[0, t], (row, right)))
        ver_copies.append(send(vertical.at[0, :, cut], ver.at[GL + 1, t], (row, left)))

    def send_rows(ref, first):
        span = pl.ds(first, GL)
        return [
            send(
                ref.at[span, :, pl.ds(8, 1), :], ref.at[span, :, pl.ds(8 + CR, 1), :], (up, col)
            ),
            send(
                ref.at[span, :, pl.ds(7 + CR, 1), :], ref.at[span, :, pl.ds(7, 1), :], (down, col)
            ),
        ]

    loaded(4, lat.at[:, :, pl.ds(8, CR), :])
    lat_copies = send_rows(lat, 0)

    for copy in row_copies + col_copies:
        copy.wait_recv()
    has_up = jnp.where(row > 0, 1.0, 0.0).astype(F32)
    has_down = jnp.where(row < NR - 1, 1.0, 0.0).astype(F32)
    side_ok = jnp.logical_or(
        jnp.logical_and(lane < 64, col < NC - 1), jnp.logical_and(lane >= 64, col > 0)
    )
    for index, ref in enumerate((p_cond, p_dem, p_leak)):
        for t in range(NT):
            cut = slice(128 * t, 128 * t + 128)
            top = stage[0, index, :, cut]
            bottom = stage[1, index, :, cut]
            if index == 0:
                top, bottom = top * has_up, bottom * has_down
            ref[t, 8:16, :] = top
            ref[t, 16 + TR : 24 + TR, :] = bottom
    for t in range(NT):
        cut = slice(128 * t, 128 * t + 128)
        p_via[t, 8:16, :] = stage_i[0, :, cut]
        p_via[t, 16 + TR : 24 + TR, :] = stage_i[1, :, cut]

    def rim(a, q, from_right, from_left):
        at = 32 * q + 8 * a
        value = jnp.where(
            lane < 64,
            pltpu.roll(from_right, (128 - at) % 128, axis=1),
            pltpu.roll(from_left, (248 - at) % 128, axis=1),
        )
        if a == 0:
            return jnp.where(side_ok, value, 0.0)
        if a == 3:
            return value.astype(jnp.int32)
        return value

    def unpack_body(i, carry):
        base = pl.multiple_of(8 * i, 8)
        from_right = pl_recv[pl.ds(8 + base, 8), :]
        from_left = pr_recv[pl.ds(8 + base, 8), :]
        for a, ref in enumerate((p_cond, p_dem, p_leak, p_via)):
            for q in range(4):
                ref[NT, pl.ds(16 + q * TQ + base, 8), :] = rim(a, q, from_right, from_left)
        return carry

    lax.fori_loop(0, TQ // 8, unpack_body, 0)
    for a, ref in enumerate((p_cond, p_dem, p_leak, p_via)):
        top = rim(a, 3, pl_recv[0:8, :], pr_recv[0:8, :])
        bottom = rim(a, 0, pl_recv[TQ + 8 : TQ + 16, :], pr_recv[TQ + 8 : TQ + 16, :])
        if a == 0:
            top, bottom = top * has_up, bottom * has_down
        ref[NT, 8:16, :] = top
        ref[NT, 16 + TR : 24 + TR, :] = bottom

    last_tile = TR // 8 + 1

    def power_coefs(c_ref, with_load):
        def coef_body(i, carry):
            base = pl.multiple_of(8 + 8 * i, 8)
            row_ok = jnp.logical_and(
                jnp.logical_or(i > 0, row > 0), jnp.logical_or(i < last_tile, row < NR - 1)
            )
            rows = pl.ds(base, 8)
            centers = [c_ref[t, rows, :] for t in range(NT + 1)]
            west, east = west_east(centers)
            for t in range(NT + 1):
                c = centers[t]
                c_n = c + c_ref[t, pl.ds(base - 1, 8), :]
                c_s = c + c_ref[t, pl.ds(base + 1, 8), :]
                c_w = c + west[t]
                c_e = c + east[t]
                denom = 0.5 * ((c_n + c_s) + (c_w + c_e)) + VIA_CONDUCT * p_via[
                    t, rows, :
                ].astype(F32)
                ok = row_ok if t < NT else jnp.logical_and(side_ok, row_ok)
                inverse = jnp.where(ok, reciprocal(denom), 0.0)
                half = 0.5 * inverse
                a_n[t, rows, :] = c_n * half
                a_s[t, rows, :] = c_s * half
                a_w[t, rows, :] = c_w * half
                a_e[t, rows, :] = c_e * half
                if with_load:
                    value = p_dem[t, rows, :] + p_leak[t, rows, :]
                    load[t, rows, :] = value
                else:
                    value = load[t, rows, :]
                b_p[t, rows, :] = value * inverse
            return carry

        lax.fori_loop(0, TR // 8 + 2, coef_body, 0)

    def power_sweep(src, dst):
        def sweep_body(j, carry):
            for i in range(2):
                base = pl.multiple_of(8 + 16 * j + 8 * i, 8)
                rows = pl.ds(base, 8)
                west, east = west_east([src[t, rows, :] for t in range(NT + 1)])
                for t in range(NT + 1):
                    dst[t, rows, :] = (
                        b_p[t, rows, :]
                        + a_n[t, rows, :] * src[t, pl.ds(base - 1, 8), :]
                        + a_s[t, rows, :] * src[t, pl.ds(base + 1, 8), :]
                    ) + (a_w[t, rows, :] * west[t] + a_e[t, rows, :] * east[t])
            return carry

        lax.fori_loop(0, TR // 16 + 1, sweep_body, 0)

    def send_heat(c_ref, d_ref, work, phase):
        def heat_body(i, carry):
            rows = pl.ds(pl.multiple_of(16 + 8 * i, 8), 8)
            for t in range(NT):
                d = d_ref[t, rows, :]
                work[t, rows, :] = load[t, rows, :] * (1.0 - d) + c_ref[t, rows, :] * d * d
            return carry

        lax.fori_loop(0, TR // 8, heat_body, 0)
        for j in range(CR // 8):
            for t in range(NT):
                total = work[t, pl.ds(16 + 64 * j, 8, stride=8), :]
                for k in range(1, 8):
                    total = total + work[t, pl.ds(16 + 64 * j + k, 8, stride=8), :]
                rows_sum[8 * j : 8 * j + 8, 128 * t : 128 * t + 128] = total
        heat = pooled(rows_sum[...], pool[...])
        heat_own[phase] = heat
        heat_all[phase, col] = heat
        return [
            send(heat_own.at[phase], heat_all.at[phase, col], (row, peer)) for peer in peers
        ]

    def thermal_coefs(layer):
        low = jnp.logical_and(layer == 0, col == 0)
        high = jnp.logical_and(layer == GL - 1, col == NC - 1)
        for i in range(CR // 8):
            rows = pl.ds(8 * i, 8)
            centers = [lat[layer, t, pl.ds(8 + 8 * i, 8), :] for t in range(NC)]
            west, east = west_east(centers)
            for t in range(NC):
                k, k_w, k_e = centers[t], west[t], east[t]
                k_n = lat[layer, t, pl.ds(7 + 8 * i, 8), :]
                k_s = lat[layer, t, pl.ds(9 + 8 * i, 8), :]
                v = ver[layer + 1, t, rows, :]
                v_b = jnp.where(low, 0.0, ver[layer, t, rows, :])
                v_a = jnp.where(high, 0.0, ver[layer + 2, t, rows, :])
                edge_n = edge_s = edge_w = edge_e = None
                if i == 0:
                    edge_n = jnp.logical_and(sub == 0, row == 0)
                    k_n = jnp.where(edge_n, 0.0, k_n)
                if i == CR // 8 - 1:
                    edge_s = jnp.logical_and(sub == 7, row == NR - 1)
                    k_s = jnp.where(edge_s, 0.0, k_s)
                if t == 0:
                    edge_w = first_lane
                    k_w = jnp.where(edge_w, 0.0, k_w)
                if t == NC - 1:
                    edge_e = last_lane
                    k_e = jnp.where(edge_e, 0.0, k_e)
                sums = [k + k_n, k + k_s, k + k_w, k + k_e, v + v_b, v + v_a]
                twice = ((sums[0] + sums[1]) + (sums[2] + sums[3])) + (sums[4] + sums[5])
                inverse = reciprocal(twice)
                t_r[layer, t, rows, :] = 2.0 * inverse
                edges = (edge_n, edge_s, edge_w, edge_e, low, high)
                for ref, total, edge in zip((t_n, t_s, t_w, t_e, t_b, t_a), sums, edges):
                    value = total * inverse
                    if edge is not None:
                        value = jnp.where(edge, 0.0, value)
                    ref[layer, t, rows, :] = value

    def sources(phase, start):
        def source_body(layer, carry):
            for i in range(CR // 8):
                rows = pl.ds(8 * i, 8)
                for t in range(NC):
                    here = layers[t, rows, :] == col * GL + layer
                    value = (
                        jnp.where(here, heat_all[phase, t, rows, :], 0.0) * t_r[layer, t, rows, :]
                    )
                    b_t[layer, t, rows, :] = value
                    if start:
                        temp_0[layer + 1, t, pl.ds(8 + 8 * i, 8), :] = value
            return carry

        lax.fori_loop(0, GL, source_body, 0)
        if start:
            for side, target, layer in ((0, 0, -1), (1, GL + 1, GL)):
                for i in range(CR // 8):
                    rows = pl.ds(8 * i, 8)
                    for t in range(NC):
                        here = layers[t, rows, :] == col * GL + layer
                        temp_0[target, t, pl.ds(8 + 8 * i, 8), :] = (
                            jnp.where(here, heat_all[phase, t, rows, :], 0.0)
                            * r_far[side, t, rows, :]
                        )

    def thermal_layer(src, dst, layer):
        for i in range(CR // 8):
            rows = pl.ds(8 * i, 8)
            mid = pl.ds(8 + 8 * i, 8)
            west, east = west_east([src[layer + 1, t, mid, :] for t in range(NC)])
            for t in range(NC):
                dst[layer + 1, t, mid, :] = (
                    (
                        b_t[layer, t, rows, :]
                        + t_n[layer, t, rows, :] * src[layer + 1, t, pl.ds(7 + 8 * i, 8), :]
                    )
                    + (
                        t_s[layer, t, rows, :] * src[layer + 1, t, pl.ds(9 + 8 * i, 8), :]
                        + t_b[layer, t, rows, :] * src[layer, t, mid, :]
                    )
                    + (
                        t_a[layer, t, rows, :] * src[layer + 2, t, mid, :]
                        + t_w[layer, t, rows, :] * west[t]
                    )
                ) + t_e[layer, t, rows, :] * east[t]

    def send_planes(ref):
        mid = pl.ds(8, CR)
        return [
            send(ref.at[GL, :, mid, :], ref.at[0, :, mid, :], (row, right)),
            send(ref.at[1, :, mid, :], ref.at[GL + 1, :, mid, :], (row, left)),
        ]

    def faces(body):
        def face_body(j, carry):
            body(j * (GL - 1))
            return carry

        lax.fori_loop(0, 2, face_body, 0)

    def interior(body):
        def interior_body(j, carry):
            body(j)
            return carry

        lax.fori_loop(1, GL - 1, interior_body, 0)

    power_coefs(p_cond, True)
    loaded(5, ver.at[pl.ds(1, GL)])
    loaded(6, layers)
    for copy in ver_copies + lat_copies:
        copy.wait_recv()
    faces(thermal_coefs)
    r_copies = [
        send(t_r.at[GL - 1], r_far.at[0], (row, right)),
        send(t_r.at[0], r_far.at[1], (row, left)),
    ]
    power_sweep(b_p, d_0)
    power_sweep(d_0, d_1)
    power_sweep(d_1, d_0)
    heat_copies = send_heat(p_cond, d_0, d_1, 0)
    interior(thermal_coefs)
    for copy in heat_copies + r_copies:
        copy.wait_recv()
    sources(0, True)
    pending = list(row_copies + col_copies + ver_copies + lat_copies + r_copies + heat_copies)

    levels = {1: send_rows(temp_0, 1)}
    in_flight = {1: levels[1]}

    def sweep(level, planes_now, rows_now):
        src, dst = (temp_0, temp_1) if level % 2 == 0 else (temp_1, temp_0)
        for copy in in_flight[level - 1]:
            copy.wait_recv()
        for copy in in_flight.pop(level - 2, []):
            copy.wait_send()
        faces(functools.partial(thermal_layer, src, dst))
        started = send_planes(dst) if planes_now else []
        interior(functools.partial(thermal_layer, src, dst))
        if rows_now:
            started += send_rows(dst, 1)
        in_flight[level] = started

    sweep(2, True, True)
    sweep(3, True, True)
    sweep(4, False, False)

    def part_body(i, carry):
        base = pl.multiple_of(8 * i, 8)
        for t in range(NC):
            ids = layers[t, pl.ds(base, 8), :] - col * GL
            total = jnp.zeros((8, 128), F32)
            for layer in range(GL):
                total = jnp.where(
                    ids == layer, temp_1[layer + 1, t, pl.ds(8 + base, 8), :], total
                )
            part[t, pl.ds(base, 8), :] = total
        return carry

    lax.fori_loop(0, CR // 8, part_body, 0)
    part_copies = [
        send(part.at[peer], part_recv.at[k], (row, peer)) for k, peer in enumerate(peers)
    ]
    in_flight[4] = send_planes(temp_1) + send_rows(temp_1, 1)
    for copy in part_copies:
        copy.wait_recv()
    total = part[col]
    for k in range(NC - 1):
        total = total + part_recv[k]
    cell[1, 8 : 8 + CR, :] = total
    own = cell.at[1, pl.ds(8, CR), :]
    low_rows = cell.at[1, pl.ds(8, 8), :]
    high_rows = cell.at[1, pl.ds(CR, 8), :]
    above, below = pl.ds(0, 8), pl.ds(8 + CR, 8)
    cell_copies = [
        send(own, cell.at[0, pl.ds(8, CR), :], (row, right)),
        send(own, cell.at[2, pl.ds(8, CR), :], (row, left)),
    ]
    for place, c in ((1, col), (0, right), (2, left)):
        cell_copies.append(send(high_rows, cell.at[place, above, :], (down, c)))
        cell_copies.append(send(low_rows, cell.at[place, below, :], (up, c)))
    for copy in cell_copies:
        copy.wait_recv()
    for target, shape in (
        (g_up, lambda x: reciprocal(1.0 + COND_SLOPE * x)),
        (e_up, lambda x: jnp.exp(LEAK_SLOPE * x)),
    ):
        coarse = shape(cell[1])
        for t in range(NT):
            target[t] = pooled(coarse, spread[t])
        from_left = jnp.broadcast_to(shape(cell[0])[:, 127:128], (CR + 16, 128))
        from_right = jnp.broadcast_to(shape(cell[2])[:, 0:1], (CR + 16, 128))
        wide = lax.broadcasted_iota(jnp.int32, (CR + 16, 128), 1)
        target[NT] = jnp.where(wide < 64, from_right, from_left)

    def warm_body(i, carry):
        rows = pl.ds(pl.multiple_of(8 + 8 * i, 8), 8)
        coarse = pl.ds(7 + i, 1)
        for t in range(NT + 1):
            c_now[t, rows, :] = p_cond[t, rows, :] * g_up[t, coarse, :]
            load[t, rows, :] = p_dem[t, rows, :] + p_leak[t, rows, :] * e_up[t, coarse, :]
        return carry

    lax.fori_loop(0, TR // 8 + 2, warm_body, 0)
    power_coefs(c_now, False)
    power_sweep(d_0, d_1)
    power_sweep(d_1, d_0)
    power_sweep(d_0, d_1)
    power_sweep(d_1, d_0)
    heat_copies = send_heat(c_now, d_0, d_1, 1)
    for t in range(NT):
        pltpu.make_async_copy(
            d_0.at[t, pl.ds(16, TR), :], drop_out.at[:, pl.ds(128 * t, 128)], out_sem.at[0]
        ).start()
    for copy in heat_copies:
        copy.wait_recv()
    sources(1, False)
    pending += part_copies + cell_copies + heat_copies
    sweep(5, True, True)
    sweep(6, True, True)
    sweep(7, True, True)
    sweep(8, False, False)
    for t in range(NC):
        pltpu.make_async_copy(
            temp_1.at[pl.ds(1, GL), t, pl.ds(8, CR), :],
            temp_out.at[:, :, pl.ds(128 * t, 128)],
            out_sem.at[1],
        ).start()
    for copies in in_flight.values():
        pending += copies
    for copy in pending:
        copy.wait_send()
    done = d_0.at[pl.ds(0, NT), pl.ds(16, TR), :]
    pltpu.make_async_copy(done, done, out_sem.at[0]).wait()
    done = temp_1.at[pl.ds(1, GL), :, pl.ds(8, CR), :]
    pltpu.make_async_copy(done, done, out_sem.at[1]).wait()


def body(num_rows, num_cols, demand, leakage, conductance, vias, layer_of, lateral_k, vertical_k):
    tile_rows, tile_cols = demand.shape
    group_layers, cell_rows, therm_cols = lateral_k.shape
    sizes = (num_rows, num_cols, tile_rows, group_layers, cell_rows)
    fine = pltpu.VMEM((9, tile_rows + 32, 128), F32)
    slab = pltpu.VMEM((group_layers, num_cols, cell_rows, 128), F32)
    coarse = (cell_rows, 128)
    hbm = pl.BlockSpec(memory_space=pl.ANY)
    return pl.pallas_call(
        functools.partial(kernel, sizes),
        out_shape=(
            jax.ShapeDtypeStruct(demand.shape, F32),
            jax.ShapeDtypeStruct(lateral_k.shape, F32),
        ),
        in_specs=[hbm] * 7,
        out_specs=(hbm, hbm),
        scratch_shapes=[fine] * 3
        + [pltpu.VMEM((9, tile_rows + 32, 128), jnp.int32)]
        + [fine] * 9
        + [
            pltpu.VMEM((2, 3, 8, tile_cols), F32),
            pltpu.VMEM((2, 8, tile_cols), jnp.int32),
            pltpu.VMEM((tile_rows // 4, 128), F32),
            pltpu.VMEM((tile_rows // 4, 128), F32),
            pltpu.VMEM((tile_rows // 4 + 16, 128), F32),
            pltpu.VMEM((tile_rows // 4 + 16, 128), F32),
            pltpu.VMEM((num_cols,) + coarse, jnp.int32),
            pltpu.VMEM((group_layers, num_cols, cell_rows + 16, 128), F32),
            pltpu.VMEM((group_layers + 2, num_cols, cell_rows, 128), F32),
        ]
        + [slab] * 8
        + [
            pltpu.VMEM((2, num_cols) + coarse, F32),
            pltpu.VMEM((group_layers + 2, num_cols, cell_rows + 16, 128), F32),
            pltpu.VMEM((group_layers + 2, num_cols, cell_rows + 16, 128), F32),
            pltpu.VMEM((tile_cols, 128), F32),
            pltpu.VMEM((8, 128, 128), F32),
            pltpu.VMEM((cell_rows, tile_cols), F32),
            pltpu.VMEM((2,) + coarse, F32),
            pltpu.VMEM((2, num_cols) + coarse, F32),
            pltpu.VMEM((num_cols,) + coarse, F32),
            pltpu.VMEM((num_cols - 1,) + coarse, F32),
            pltpu.VMEM((3, cell_rows + 16, 128), F32),
            pltpu.VMEM((9, cell_rows + 16, 128), F32),
            pltpu.VMEM((9, cell_rows + 16, 128), F32),
            pltpu.SemaphoreType.DMA((7,)),
            pltpu.SemaphoreType.DMA((2,)),
            pltpu.SemaphoreType.DMA((LINKS,)),
            pltpu.SemaphoreType.DMA((LINKS,)),
        ],
        compiler_params=pltpu.CompilerParams(
            collective_id=0, has_side_effects=True, vmem_limit_bytes=52 << 20
        ),
        name="coupled",
    )(demand, leakage, conductance, vias, layer_of, lateral_k, vertical_k)


def solution(mesh):
    in_specs = (
        P("row", "col"),
        P("row", "col"),
        P("row", "col"),
        P("row", "col"),
        P("row", None),
        P("col", "row", None),
        P("col", "row", None),
    )
    out_specs = (P("row", "col"), P("col", "row", None))
    step = functools.partial(body, mesh.shape["row"], mesh.shape["col"])
    return jax.shard_map(step, mesh=mesh, in_specs=in_specs, out_specs=out_specs, check_vma=False)
```

time: 599 us -> 110 us (0.18)
  the two profiles are of different devices: /device:TPU:23 before, /device:TPU:0 now
where the time goes in v1:
time: 110 us; the launch traced here: 109 us
  Pallas kernels  105 us (95%)
  local copies, waits for them, and re-layouts  3.46 us (3%)
    pallas_call x1, Pallas kernels, body(): pl.pallas_call(functools.partial(kernel, sizes), out_shape=(jax.ShapeDtyp...  105 us
    unnamed x6, local copies, waits for them, and re-layouts  3.46 us

profile of v1, /device:TPU:0, one launch (start us, length us, event | category | flops | bytes accessed | tf_op | source)
XLA Modules:
  0.0 108.8 jit_solution(10206226230190018873)
XLA Ops:
  0.6 0.0 copy-start
  0.6 0.9 copy-done
  1.5 104.7 %coupled.1 = (f32[256,1024]{1,0:T(8,128)S(1)}, f32[8,32,1024]{2,1,0:T(8,128)}) custom-call(f32[256,1024]{1,0:T(8,128)} %demand.1, f32[256,1024]{1,0:T(8,128)} %leakage.1, f32[256,1024]{1,0:T(8,128)} %conductance.1, s32[256,1024]{1,0:T(8,128)} %vias.1, s32[32,1024]{1,0:T(8,128)S(1)} %copy-done, f32[8,32,1024]{2,1,0:T(8,128)} %lateral.1, f32[8,32,1024]{2,1,0:T(8,128)} %vertical.1), custom_call_target="tpu_custom_call" | custom-call | tf_op jit(solution)/shard_map/coupled/pallas_call | solution.py:587
  106.3 0.0 copy-start.1
  106.3 1.0 copy.11
  107.3 0.6 copy-done.1
  107.9 1.0 copy.12
Async XLA Ops:
  0.6 0.9 copy-start
  106.3 1.6 %copy-start.1 = (f32[8,32,1024]{2,1,0:T(8,128)S(1)}, f32[8,32,1024]{2,1,0:T(8,128)}, u32[]{:S(2)}) copy-start(f32[8,32,1024]{2,1,0:T(8,128)} %get-tuple-element.5) | copy-start | bytes 3145732

commit v2 on v1

--- a/solution.py
+++ b/solution.py
@@ -15,9 +15,11 @@
 VIA_CONDUCT = 4.0
 
 MESH = pl.DeviceIdType.MESH
-HIGH = lax.Precision.HIGHEST
 F32 = jnp.float32
+BF16 = jnp.bfloat16
 LINKS = 128
+COEF_TILES = 4
+HALVES = 2
 
 
 def reciprocal(value):
@@ -25,7 +27,15 @@
 
 
 def pooled(left, right):
-    return jnp.dot(left, right, precision=HIGH, preferred_element_type=F32)
+    parts = []
+    for _ in range(3):
+        part = left.astype(BF16).astype(F32)
+        parts.append(part)
+        left = left - part
+    count = left.shape[0]
+    stacked = jnp.concatenate(parts, axis=0).astype(BF16)
+    product = jnp.dot(stacked, right, preferred_element_type=F32)
+    return (product[2 * count :] + product[count : 2 * count]) + product[:count]
 
 
 def kernel(
@@ -75,6 +85,8 @@
     pool,
     spread,
     rows_sum,
+    rim_send,
+    rim_recv,
     heat_own,
     heat_all,
     part,
@@ -83,7 +95,6 @@
     g_up,
     e_up,
     load_sem,
-    out_sem,
     send_sem,
     recv_sem,
 ):
@@ -124,12 +135,22 @@
         east = [jnp.where(last_lane, minus[(t + 1) % n], minus[t]) for t in range(n)]
         return west, east
 
+    barrier = pltpu.get_barrier_semaphore()
+    near = [(row, p) for p in peers]
+    near += [(r, c) for r in (up, down) for c in (col, left, right)]
+    for device in near:
+        pl.semaphore_signal(barrier, inc=1, device_id=device, device_id_type=MESH)
+
     power = ((conductance, p_cond), (demand, p_dem), (leakage, p_leak), (vias, p_via))
-    for index, (src, dst) in enumerate(power):
-        for t in range(NT):
-            pltpu.make_async_copy(
-                src.at[:, pl.ds(128 * t, 128)], dst.at[t, pl.ds(16, TR), :], load_sem.at[index]
-            ).start()
+    outer_tiles, inner_tiles = (0, NT - 1), tuple(range(1, NT - 1))
+    for offset, tiles in ((0, outer_tiles), (7, inner_tiles)):
+        for index, (src, dst) in enumerate(power):
+            for t in tiles:
+                pltpu.make_async_copy(
+                    src.at[:, pl.ds(128 * t, 128)],
+                    dst.at[t, pl.ds(16, TR), :],
+                    load_sem.at[offset + index],
+                ).start()
     for t in range(NC):
         cut = pl.ds(128 * t, 128)
         pltpu.make_async_copy(
@@ -143,11 +164,6 @@
     def loaded(index, ref):
         pltpu.make_async_copy(ref, ref, load_sem.at[index]).wait()
 
-    barrier = pltpu.get_barrier_semaphore()
-    near = [(row, p) for p in peers]
-    near += [(r, c) for r in (up, down) for c in (col, left, right)]
-    for device in near:
-        pl.semaphore_signal(barrier, inc=1, device_id=device, device_id_type=MESH)
     pl.semaphore_wait(barrier, len(near))
 
     row_copies = []
@@ -155,20 +171,9 @@
         for side, start, device in ((0, TR - 8, (down, col)), (1, 0, (up, col))):
             dst = stage_i.at[side] if index == 3 else stage.at[side, index]
             row_copies.append(send(src.at[pl.ds(start, 8), :], dst, device))
-    ver_copies = []
-
-    def pool_body(i, carry):
-        r = lax.broadcasted_iota(jnp.int32, (128, 128), 0)
-        c = lax.broadcasted_iota(jnp.int32, (128, 128), 1)
-        start = pl.multiple_of(i * 128, 128)
-        pool[pl.ds(start, 128), :] = jnp.where(16 * i + r // 8 == c, 1.0 / 64.0, 0.0)
-        spread[i] = jnp.where(16 * i + c // 8 == r, 1.0, 0.0)
-        return carry
-
-    lax.fori_loop(0, NT, pool_body, 0)
 
     for index, (_, dst) in enumerate(power):
-        loaded(index, dst.at[pl.ds(0, NT), pl.ds(16, TR), :])
+        loaded(index, dst.at[pl.ds(0, 2), pl.ds(16, TR), :])
 
     def pack_body(i, carry):
         base = pl.multiple_of(8 * i, 8)
@@ -193,11 +198,6 @@
         col_copies.append(send(src.at[pl.ds(TQ - 8, 8), :], dst.at[pl.ds(0, 8), :], (down, c)))
         col_copies.append(send(src.at[pl.ds(0, 8), :], dst.at[pl.ds(TQ + 8, 8), :], (up, c)))
 
-    for t in range(NC):
-        cut = pl.ds(128 * t, 128)
-        ver_copies.append(send(vertical.at[GL - 1, :, cut], ver.at[0, t], (row, right)))
-        ver_copies.append(send(vertical.at[0, :, cut], ver.at[GL + 1, t], (row, left)))
-
     def send_rows(ref, first):
         span = pl.ds(first, GL)
         return [
@@ -211,6 +211,23 @@
 
     loaded(4, lat.at[:, :, pl.ds(8, CR), :])
     lat_copies = send_rows(lat, 0)
+    ver_copies = []
+    for t in range(NC):
+        cut = pl.ds(128 * t, 128)
+        ver_copies.append(send(vertical.at[GL - 1, :, cut], ver.at[0, t], (row, right)))
+        ver_copies.append(send(vertical.at[0, :, cut], ver.at[GL + 1, t], (row, left)))
+
+    def pool_body(i, carry):
+        r = lax.broadcasted_iota(jnp.int32, (128, 128), 0)
+        c = lax.broadcasted_iota(jnp.int32, (128, 128), 1)
+        start = pl.multiple_of(i * 128, 128)
+        pool[pl.ds(start, 128), :] = jnp.where(16 * i + r // 8 == c, 1.0 / 64.0, 0.0).astype(BF16)
+        spread[i] = jnp.where(16 * i + c // 8 == r, 1.0, 0.0).astype(BF16)
+        return carry
+
+    lax.fori_loop(0, NT, pool_body, 0)
+    for index, (_, dst) in enumerate(power):
+        loaded(7 + index, dst.at[pl.ds(1, NT - 2), pl.ds(16, TR), :])
 
     for copy in row_copies + col_copies:
         copy.wait_recv()
@@ -267,7 +284,7 @@
     last_tile = TR // 8 + 1
 
     def power_coefs(c_ref, with_load):
-        def coef_body(i, carry):
+        def coef_tile(i):
             base = pl.multiple_of(8 + 8 * i, 8)
             row_ok = jnp.logical_and(
                 jnp.logical_or(i > 0, row > 0), jnp.logical_or(i < last_tile, row < NR - 1)
@@ -297,14 +314,20 @@
                 else:
                     value = load[t, rows, :]
                 b_p[t, rows, :] = value * inverse
-            return carry
-
-        lax.fori_loop(0, TR // 8 + 2, coef_body, 0)
+
+        def coef_body(j, carry):
+            for k in range(COEF_TILES):
+                coef_tile(COEF_TILES * j + k)
+            return carry
+
+        lax.fori_loop(0, pl.cdiv(TR // 8 + 2, COEF_TILES), coef_body, 0)
 
     def power_sweep(src, dst):
+        per = (TR // 8 + 2) // HALVES
+
         def sweep_body(j, carry):
-            for i in range(2):
-                base = pl.multiple_of(8 + 16 * j + 8 * i, 8)
+            for i in range(per):
+                base = pl.multiple_of(8 + 8 * (per * j + i), 8)
                 rows = pl.ds(base, 8)
                 west, east = west_east([src[t, rows, :] for t in range(NT + 1)])
                 for t in range(NT + 1):
@@ -315,17 +338,21 @@
                     ) + (a_w[t, rows, :] * west[t] + a_e[t, rows, :] * east[t])
             return carry
 
-        lax.fori_loop(0, TR // 16 + 1, sweep_body, 0)
+        lax.fori_loop(0, HALVES, sweep_body, 0)
 
     def send_heat(c_ref, d_ref, work, phase):
         def heat_body(i, carry):
-            rows = pl.ds(pl.multiple_of(16 + 8 * i, 8), 8)
-            for t in range(NT):
-                d = d_ref[t, rows, :]
-                work[t, rows, :] = load[t, rows, :] * (1.0 - d) + c_ref[t, rows, :] * d * d
-            return carry
-
-        lax.fori_loop(0, TR // 8, heat_body, 0)
+            for k in range(4):
+                rows = pl.ds(pl.multiple_of(16 + 32 * i + 8 * k, 8), 8)
+                for t in range(NT):
+                    d = d_ref[t, rows, :]
+                    work[t, rows, :] = load[t, rows, :] * (1.0 - d) + c_ref[t, rows, :] * d * d
+                    if phase == 1:
+                        out_rows = pl.ds(pl.multiple_of(32 * i + 8 * k, 8), 8)
+                        drop_out[out_rows, 128 * t : 128 * t + 128] = d
+            return carry
+
+        lax.fori_loop(0, TR // 32, heat_body, 0)
         for j in range(CR // 8):
             for t in range(NT):
                 total = work[t, pl.ds(16 + 64 * j, 8, stride=8), :]
@@ -403,33 +430,94 @@
                             * r_far[side, t, rows, :]
                         )
 
-    def thermal_layer(src, dst, layer):
-        for i in range(CR // 8):
-            rows = pl.ds(8 * i, 8)
-            mid = pl.ds(8 + 8 * i, 8)
-            west, east = west_east([src[layer + 1, t, mid, :] for t in range(NC)])
+    half = NC // 2
+    chunks = (range(half), range(half, NC))
+    tall = CR // 8
+    edge_tiles = sorted({0, tall - 1})
+    mid_tiles = [i for i in range(tall) if i not in edge_tiles]
+
+    def thermal_block(src, dst, first, depth, row_tiles, tiles, out=None):
+        cache = {}
+
+        def at(k, i, t):
+            if (k, i, t) not in cache:
+                cache[k, i, t] = src[first + k, t, pl.ds(8 + 8 * i, 8), :]
+            return cache[k, i, t]
+
+        for k in range(depth):
+            layer = first + k
+            for i in row_tiles:
+                rows = pl.ds(8 * i, 8)
+                plus = {
+                    t: pltpu.roll(at(k + 1, i, t), 1, axis=1)
+                    for t in range(max(tiles[0] - 1, 0), tiles[-1] + 1)
+                }
+                minus = {
+                    t: pltpu.roll(at(k + 1, i, t), 127, axis=1)
+                    for t in range(tiles[0], min(tiles[-1] + 2, NC))
+                }
+                for t in tiles:
+                    west = plus[t] if t == 0 else jnp.where(first_lane, plus[t - 1], plus[t])
+                    east = minus[t] if t == NC - 1 else jnp.where(last_lane, minus[t + 1], minus[t])
+                    value = (
+                        (
+                            b_t[layer, t, rows, :]
+                            + t_n[layer, t, rows, :] * src[layer + 1, t, pl.ds(7 + 8 * i, 8), :]
+                        )
+                        + (
+                            t_s[layer, t, rows, :] * src[layer + 1, t, pl.ds(9 + 8 * i, 8), :]
+                            + t_b[layer, t, rows, :] * at(k, i, t)
+                        )
+                        + (t_a[layer, t, rows, :] * at(k + 2, i, t))
+                        + (t_w[layer, t, rows, :] * west + t_e[layer, t, rows, :] * east)
+                    )
+                    if out is None:
+                        dst[layer + 1, t, pl.ds(8 + 8 * i, 8), :] = value
+                    else:
+                        out[layer, rows, 128 * t : 128 * t + 128] = value
+
+    def inner_layers(src, dst, row_tiles, out=None):
+        depth = (GL - 2) // 2
+
+        def inner_body(j, carry):
+            thermal_block(src, dst, 1 + depth * j, depth, row_tiles, range(NC), out)
+            return carry
+
+        if row_tiles:
+            lax.fori_loop(0, 2, inner_body, 0)
+
+    def send_planes(ref, chunk):
+        mid, tiles = pl.ds(8, CR), pl.ds(chunk[0], len(chunk))
+        return [
+            send(ref.at[GL, tiles, mid, :], ref.at[0, tiles, mid, :], (row, right)),
+            send(ref.at[1, tiles, mid, :], ref.at[GL + 1, tiles, mid, :], (row, left)),
+        ]
+
+    def send_rims(ref, level):
+        def rim_body(layer, carry):
             for t in range(NC):
-                dst[layer + 1, t, mid, :] = (
-                    (
-                        b_t[layer, t, rows, :]
-                        + t_n[layer, t, rows, :] * src[layer + 1, t, pl.ds(7 + 8 * i, 8), :]
-                    )
-                    + (
-                        t_s[layer, t, rows, :] * src[layer + 1, t, pl.ds(9 + 8 * i, 8), :]
-                        + t_b[layer, t, rows, :] * src[layer, t, mid, :]
-                    )
-                    + (
-                        t_a[layer, t, rows, :] * src[layer + 2, t, mid, :]
-                        + t_w[layer, t, rows, :] * west[t]
-                    )
-                ) + t_e[layer, t, rows, :] * east[t]
-
-    def send_planes(ref):
-        mid = pl.ds(8, CR)
+                rim_send[level - 1, 0, t, pl.ds(layer, 1), :] = ref[layer + 1, t, pl.ds(8, 1), :]
+                rim_send[level - 1, 1, t, pl.ds(layer, 1), :] = ref[
+                    layer + 1, t, pl.ds(7 + CR, 1), :
+                ]
+            return carry
+
+        lax.fori_loop(0, GL, rim_body, 0)
         return [
-            send(ref.at[GL, :, mid, :], ref.at[0, :, mid, :], (row, right)),
-            send(ref.at[1, :, mid, :], ref.at[GL + 1, :, mid, :], (row, left)),
+            send(rim_send.at[level - 1, side], rim_recv.at[level - 1, side], (r, col))
+            for side, r in ((0, up), (1, down))
         ]
+
+    def place_rims(ref, level):
+        def place_body(layer, carry):
+            for t in range(NC):
+                ref[layer + 1, t, pl.ds(8 + CR, 1), :] = rim_recv[
+                    level - 1, 0, t, pl.ds(layer, 1), :
+                ]
+                ref[layer + 1, t, pl.ds(7, 1), :] = rim_recv[level - 1, 1, t, pl.ds(layer, 1), :]
+            return carry
+
+        lax.fori_loop(0, GL, place_body, 0)
 
     def faces(body):
         def face_body(j, carry):
@@ -465,25 +553,37 @@
     sources(0, True)
     pending = list(row_copies + col_copies + ver_copies + lat_copies + r_copies + heat_copies)
 
-    levels = {1: send_rows(temp_0, 1)}
-    in_flight = {1: levels[1]}
-
-    def sweep(level, planes_now, rows_now):
+    rims = {1: send_rims(temp_0, 1)}
+    planes = {}
+
+    def sweep(level, exchange=True, out=None):
         src, dst = (temp_0, temp_1) if level % 2 == 0 else (temp_1, temp_0)
-        for copy in in_flight[level - 1]:
+        for copies in planes.get(level - 2, ()):
+            for copy in copies:
+                copy.wait_send()
+        for copy in rims[level - 1]:
             copy.wait_recv()
-        for copy in in_flight.pop(level - 2, []):
-            copy.wait_send()
-        faces(functools.partial(thermal_layer, src, dst))
-        started = send_planes(dst) if planes_now else []
-        interior(functools.partial(thermal_layer, src, dst))
-        if rows_now:
-            started += send_rows(dst, 1)
-        in_flight[level] = started
-
-    sweep(2, True, True)
-    sweep(3, True, True)
-    sweep(4, False, False)
+        place_rims(src, level - 1)
+        sent = []
+        for index, chunk in enumerate(chunks):
+            if level - 1 in planes:
+                for copy in planes[level - 1][index]:
+                    copy.wait_recv()
+            for layer in (0, GL - 1):
+                thermal_block(src, dst, layer, 1, range(tall), chunk, out)
+            if exchange:
+                sent.append(send_planes(dst, chunk))
+        if exchange:
+            planes[level] = sent
+            inner_layers(src, dst, edge_tiles)
+            rims[level] = send_rims(dst, level)
+            inner_layers(src, dst, mid_tiles)
+        else:
+            inner_layers(src, dst, list(range(tall)), out)
+
+    sweep(2)
+    sweep(3)
+    sweep(4, False)
 
     def part_body(i, carry):
         base = pl.multiple_of(8 * i, 8)
@@ -501,7 +601,8 @@
     part_copies = [
         send(part.at[peer], part_recv.at[k], (row, peer)) for k, peer in enumerate(peers)
     ]
-    in_flight[4] = send_planes(temp_1) + send_rows(temp_1, 1)
+    rims[4] = send_rims(temp_1, 4)
+    planes[4] = [send_planes(temp_1, chunk) for chunk in chunks]
     for copy in part_copies:
         copy.wait_recv()
     total = part[col]
@@ -519,68 +620,77 @@
     for place, c in ((1, col), (0, right), (2, left)):
         cell_copies.append(send(high_rows, cell.at[place, above, :], (down, c)))
         cell_copies.append(send(low_rows, cell.at[place, below, :], (up, c)))
+    shapes = (
+        (g_up, lambda x: reciprocal(1.0 + COND_SLOPE * x)),
+        (e_up, lambda x: jnp.exp(LEAK_SLOPE * x)),
+    )
+    for target, shape in shapes:
+        coarse = shape(total)
+        for t in range(NT):
+            target[t, 8 : 8 + CR, :] = pooled(coarse, spread[t])
+
+    def warm_tile(i, tiles):
+        rows = pl.ds(pl.multiple_of(8 + 8 * i, 8), 8)
+        coarse = pl.ds(7 + i, 1)
+        for t in tiles:
+            c_now[t, rows, :] = p_cond[t, rows, :] * g_up[t, coarse, :]
+            load[t, rows, :] = p_dem[t, rows, :] + p_leak[t, rows, :] * e_up[t, coarse, :]
+
+    def warm_body(j, carry):
+        for k in range(4):
+            warm_tile(1 + 4 * j + k, range(NT))
+        return carry
+
+    lax.fori_loop(0, TR // 32, warm_body, 0)
     for copy in cell_copies:
         copy.wait_recv()
-    for target, shape in (
-        (g_up, lambda x: reciprocal(1.0 + COND_SLOPE * x)),
-        (e_up, lambda x: jnp.exp(LEAK_SLOPE * x)),
-    ):
-        coarse = shape(cell[1])
+    for target, shape in shapes:
+        coarse = shape(jnp.concatenate([cell[1, 0:8, :], cell[1, 8 + CR : 16 + CR, :]], axis=0))
         for t in range(NT):
-            target[t] = pooled(coarse, spread[t])
+            rims_up = pooled(coarse, spread[t])
+            target[t, 0:8, :] = rims_up[0:8]
+            target[t, 8 + CR : 16 + CR, :] = rims_up[8:16]
         from_left = jnp.broadcast_to(shape(cell[0])[:, 127:128], (CR + 16, 128))
         from_right = jnp.broadcast_to(shape(cell[2])[:, 0:1], (CR + 16, 128))
         wide = lax.broadcasted_iota(jnp.int32, (CR + 16, 128), 1)
         target[NT] = jnp.where(wide < 64, from_right, from_left)
-
-    def warm_body(i, carry):
-        rows = pl.ds(pl.multiple_of(8 + 8 * i, 8), 8)
-        coarse = pl.ds(7 + i, 1)
-        for t in range(NT + 1):
-            c_now[t, rows, :] = p_cond[t, rows, :] * g_up[t, coarse, :]
-            load[t, rows, :] = p_dem[t, rows, :] + p_leak[t, rows, :] * e_up[t, coarse, :]
+    warm_tile(0, range(NT))
+    warm_tile(last_tile, range(NT))
+
+    def warm_side_body(j, carry):
+        for k in range(2):
+            warm_tile(2 * j + k, (NT,))
         return carry
 
-    lax.fori_loop(0, TR // 8 + 2, warm_body, 0)
+    lax.fori_loop(0, TR // 16 + 1, warm_side_body, 0)
+
     power_coefs(c_now, False)
     power_sweep(d_0, d_1)
     power_sweep(d_1, d_0)
     power_sweep(d_0, d_1)
     power_sweep(d_1, d_0)
     heat_copies = send_heat(c_now, d_0, d_1, 1)
-    for t in range(NT):
-        pltpu.make_async_copy(
-            d_0.at[t, pl.ds(16, TR), :], drop_out.at[:, pl.ds(128 * t, 128)], out_sem.at[0]
-        ).start()
     for copy in heat_copies:
         copy.wait_recv()
     sources(1, False)
     pending += part_copies + cell_copies + heat_copies
-    sweep(5, True, True)
-    sweep(6, True, True)
-    sweep(7, True, True)
-    sweep(8, False, False)
-    for t in range(NC):
-        pltpu.make_async_copy(
-            temp_1.at[pl.ds(1, GL), t, pl.ds(8, CR), :],
-            temp_out.at[:, :, pl.ds(128 * t, 128)],
-            out_sem.at[1],
-        ).start()
-    for copies in in_flight.values():
+    sweep(5)
+    sweep(6)
+    sweep(7)
+    sweep(8, False, temp_out)
+    for copies in rims.values():
+        pending += copies
+    for copies in planes[7]:
         pending += copies
     for copy in pending:
         copy.wait_send()
-    done = d_0.at[pl.ds(0, NT), pl.ds(16, TR), :]
-    pltpu.make_async_copy(done, done, out_sem.at[0]).wait()
-    done = temp_1.at[pl.ds(1, GL), :, pl.ds(8, CR), :]
-    pltpu.make_async_copy(done, done, out_sem.at[1]).wait()
 
 
 def body(num_rows, num_cols, demand, leakage, conductance, vias, layer_of, lateral_k, vertical_k):
     tile_rows, tile_cols = demand.shape
     group_layers, cell_rows, therm_cols = lateral_k.shape
     sizes = (num_rows, num_cols, tile_rows, group_layers, cell_rows)
-    fine = pltpu.VMEM((9, tile_rows + 32, 128), F32)
+    fine = pltpu.VMEM((9, tile_rows + 48, 128), F32)
     slab = pltpu.VMEM((group_layers, num_cols, cell_rows, 128), F32)
     coarse = (cell_rows, 128)
     hbm = pl.BlockSpec(memory_space=pl.ANY)
@@ -591,9 +701,9 @@
             jax.ShapeDtypeStruct(lateral_k.shape, F32),
         ),
         in_specs=[hbm] * 7,
-        out_specs=(hbm, hbm),
+        out_specs=(pl.BlockSpec(memory_space=pltpu.VMEM),) * 2,
         scratch_shapes=[fine] * 3
-        + [pltpu.VMEM((9, tile_rows + 32, 128), jnp.int32)]
+        + [pltpu.VMEM((9, tile_rows + 48, 128), jnp.int32)]
         + [fine] * 9
         + [
             pltpu.VMEM((2, 3, 8, tile_cols), F32),
@@ -611,9 +721,11 @@
             pltpu.VMEM((2, num_cols) + coarse, F32),
             pltpu.VMEM((group_layers + 2, num_cols, cell_rows + 16, 128), F32),
             pltpu.VMEM((group_layers + 2, num_cols, cell_rows + 16, 128), F32),
-            pltpu.VMEM((tile_cols, 128), F32),
-            pltpu.VMEM((8, 128, 128), F32),
+            pltpu.VMEM((tile_cols, 128), BF16),
+            pltpu.VMEM((8, 128, 128), BF16),
             pltpu.VMEM((cell_rows, tile_cols), F32),
+            pltpu.VMEM((7, 2, num_cols, group_layers, 128), F32),
+            pltpu.VMEM((7, 2, num_cols, group_layers, 128), F32),
             pltpu.VMEM((2,) + coarse, F32),
             pltpu.VMEM((2, num_cols) + coarse, F32),
             pltpu.VMEM((num_cols,) + coarse, F32),
@@ -621,8 +733,7 @@
             pltpu.VMEM((3, cell_rows + 16, 128), F32),
             pltpu.VMEM((9, cell_rows + 16, 128), F32),
             pltpu.VMEM((9, cell_rows + 16, 128), F32),
-            pltpu.SemaphoreType.DMA((7,)),
-            pltpu.SemaphoreType.DMA((2,)),
+            pltpu.SemaphoreType.DMA((11,)),
             pltpu.SemaphoreType.DMA((LINKS,)),
             pltpu.SemaphoreType.DMA((LINKS,)),
         ],

time: 110 us -> 93.4 us (0.85)
  the two profiles are of different devices: /device:TPU:0 before, /device:TPU:8 now
where the time goes in v2:
time: 93.4 us; the launch traced here: 93.3 us
  Pallas kernels  89.1 us (95%)
  local copies, waits for them, and re-layouts  3.46 us (4%)
    pallas_call x1, Pallas kernels, body(): pl.pallas_call(functools.partial(kernel, sizes), out_shape=(jax.ShapeDtyp...  89.1 us
    unnamed x6, local copies, waits for them, and re-layouts  3.46 us

profile of v2, /device:TPU:8, one launch (start us, length us, event | category | flops | bytes accessed | tf_op | source)
XLA Modules:
  0.0 93.3 jit_solution(12961171969710279910)
XLA Ops:
  0.6 0.0 copy-start
  0.6 0.9 copy-done
  1.5 89.1 %coupled.1 = (f32[256,1024]{1,0:T(8,128)S(1)}, f32[8,32,1024]{2,1,0:T(8,128)}) custom-call(f32[256,1024]{1,0:T(8,128)} %demand.1, f32[256,1024]{1,0:T(8,128)} %leakage.1, f32[256,1024]{1,0:T(8,128)} %conductance.1, s32[256,1024]{1,0:T(8,128)} %vias.1, s32[32,1024]{1,0:T(8,128)S(1)} %copy-done, f32[8,32,1024]{2,1,0:T(8,128)} %lateral.1, f32[8,32,1024]{2,1,0:T(8,128)} %vertical.1), custom_call_target="tpu_custom_call" | custom-call | tf_op jit(solution)/shard_map/coupled/pallas_call | solution.py:697
  90.7 0.0 copy-start.1
  90.7 1.0 %copy.11 = f32[256,1024]{1,0:T(8,128)} copy(f32[256,1024]{1,0:T(8,128)S(1)} %get-tuple-element.4) | data formatting | bytes 2097152
  91.7 0.6 copy-done.1
  92.3 1.0 %copy.12 = f32[8,32,1024]{2,1,0:T(8,128)} copy(f32[8,32,1024]{2,1,0:T(8,128)S(1)} %copy-done.1) | data formatting | bytes 2097152
Async XLA Ops:
  0.6 0.9 copy-start
  90.7 1.6 %copy-start.1 = (f32[8,32,1024]{2,1,0:T(8,128)S(1)}, f32[8,32,1024]{2,1,0:T(8,128)}, u32[]{:S(2)}) copy-start(f32[8,32,1024]{2,1,0:T(8,128)} %get-tuple-element.5) | copy-start | bytes 3145732

commit v3 on v2

--- a/solution.py
+++ b/solution.py
@@ -79,14 +79,11 @@
     t_a,
     t_r,
     b_t,
-    r_far,
     temp_0,
     temp_1,
     pool,
     spread,
     rows_sum,
-    rim_send,
-    rim_recv,
     heat_own,
     heat_all,
     part,
@@ -137,7 +134,7 @@
 
     barrier = pltpu.get_barrier_semaphore()
     near = [(row, p) for p in peers]
-    near += [(r, c) for r in (up, down) for c in (col, left, right)]
+    near += [(r, c) for r in (up, down) for c in (col, *peers)]
     for device in near:
         pl.semaphore_signal(barrier, inc=1, device_id=device, device_id_type=MESH)
 
@@ -154,23 +151,15 @@
     for t in range(NC):
         cut = pl.ds(128 * t, 128)
         pltpu.make_async_copy(
-            lateral.at[:, :, cut], lat.at[:, t, pl.ds(8, CR), :], load_sem.at[4]
+            lateral.at[:, :, cut], lat.at[pl.ds(4, GL), t, pl.ds(12, CR), :], load_sem.at[4]
         ).start()
         pltpu.make_async_copy(
-            vertical.at[:, :, cut], ver.at[pl.ds(1, GL), t], load_sem.at[5]
+            vertical.at[:, :, cut], ver.at[pl.ds(4, GL), t, pl.ds(4, CR), :], load_sem.at[5]
         ).start()
-        pltpu.make_async_copy(layer_of.at[:, cut], layers.at[t], load_sem.at[6]).start()
+        pltpu.make_async_copy(layer_of.at[:, cut], layers.at[t, pl.ds(8, CR), :], load_sem.at[6]).start()
 
     def loaded(index, ref):
         pltpu.make_async_copy(ref, ref, load_sem.at[index]).wait()
-
-    pl.semaphore_wait(barrier, len(near))
-
-    row_copies = []
-    for index, src in enumerate((conductance, demand, leakage, vias)):
-        for side, start, device in ((0, TR - 8, (down, col)), (1, 0, (up, col))):
-            dst = stage_i.at[side] if index == 3 else stage.at[side, index]
-            row_copies.append(send(src.at[pl.ds(start, 8), :], dst, device))
 
     for index, (_, dst) in enumerate(power):
         loaded(index, dst.at[pl.ds(0, 2), pl.ds(16, TR), :])
@@ -192,30 +181,46 @@
         return carry
 
     lax.fori_loop(0, TQ // 8, pack_body, 0)
+    pl.semaphore_wait(barrier, len(near))
+
+    row_copies = []
+    for index, src in enumerate((conductance, demand, leakage, vias)):
+        for side, start, device in ((0, TR - 8, (down, col)), (1, 0, (up, col))):
+            dst = stage_i.at[side] if index == 3 else stage.at[side, index]
+            row_copies.append(send(src.at[pl.ds(start, 8), :], dst, device))
+
     col_copies = []
     for src, dst, c in ((pl_send, pl_recv, left), (pr_send, pr_recv, right)):
         col_copies.append(send(src, dst.at[pl.ds(8, TQ), :], (row, c)))
         col_copies.append(send(src.at[pl.ds(TQ - 8, 8), :], dst.at[pl.ds(0, 8), :], (down, c)))
         col_copies.append(send(src.at[pl.ds(0, 8), :], dst.at[pl.ds(TQ + 8, 8), :], (up, c)))
 
-    def send_rows(ref, first):
-        span = pl.ds(first, GL)
-        return [
-            send(
-                ref.at[span, :, pl.ds(8, 1), :], ref.at[span, :, pl.ds(8 + CR, 1), :], (up, col)
-            ),
-            send(
-                ref.at[span, :, pl.ds(7 + CR, 1), :], ref.at[span, :, pl.ds(7, 1), :], (down, col)
-            ),
-        ]
-
-    loaded(4, lat.at[:, :, pl.ds(8, CR), :])
-    lat_copies = send_rows(lat, 0)
-    ver_copies = []
-    for t in range(NC):
-        cut = pl.ds(128 * t, 128)
-        ver_copies.append(send(vertical.at[GL - 1, :, cut], ver.at[0, t], (row, right)))
-        ver_copies.append(send(vertical.at[0, :, cut], ver.at[GL + 1, t], (row, left)))
+    def send_rim(ref, first, depth, sides=((-1, 0), (1, 0), (0, 1), (0, -1), (1, 1), (1, -1), (-1, 1), (-1, -1))):
+        layer_spans = {1: (GL + 4 - depth, 4 - depth, depth), -1: (4, GL + 4, depth), 0: (4, 4, GL)}
+        row_spans = {1: (first + CR - 4, first - 4, 4), -1: (first, first + CR, 4), 0: (first, first, CR)}
+        copies = []
+        for by_row, by_col in sides:
+            from_layer, to_layer, count_layers = layer_spans[by_col]
+            from_row, to_row, count_rows = row_spans[by_row]
+            device = ((up, row, down)[by_row + 1], (left, col, right)[by_col + 1])
+            copies.append(
+                send(
+                    ref.at[pl.ds(from_layer, count_layers), :, pl.ds(from_row, count_rows), :],
+                    ref.at[pl.ds(to_layer, count_layers), :, pl.ds(to_row, count_rows), :],
+                    device,
+                )
+            )
+        return copies
+
+    loaded(4, lat.at[pl.ds(4, GL), :, pl.ds(12, CR), :])
+    loaded(5, ver.at[pl.ds(4, GL), :, pl.ds(4, CR), :])
+    loaded(6, layers.at[:, pl.ds(8, CR), :])
+    lat_copies = send_rim(lat, 12, 3)
+    ver_copies = send_rim(ver, 4, 4)
+    layer_copies = [
+        send(layers.at[:, pl.ds(8, 8), :], layers.at[:, pl.ds(8 + CR, 8), :], (up, col)),
+        send(layers.at[:, pl.ds(CR, 8), :], layers.at[:, pl.ds(0, 8), :], (down, col)),
+    ]
 
     def pool_body(i, carry):
         r = lax.broadcasted_iota(jnp.int32, (128, 128), 0)
@@ -361,31 +366,44 @@
                 rows_sum[8 * j : 8 * j + 8, 128 * t : 128 * t + 128] = total
         heat = pooled(rows_sum[...], pool[...])
         heat_own[phase] = heat
-        heat_all[phase, col] = heat
-        return [
-            send(heat_own.at[phase], heat_all.at[phase, col], (row, peer)) for peer in peers
+        heat_all[phase, col, 8 : 8 + CR, :] = heat
+        copies = [
+            send(heat_own.at[phase], heat_all.at[phase, col, pl.ds(8, CR), :], (row, peer))
+            for peer in peers
         ]
-
-    def thermal_coefs(layer):
-        low = jnp.logical_and(layer == 0, col == 0)
-        high = jnp.logical_and(layer == GL - 1, col == NC - 1)
-        for i in range(CR // 8):
+        for c in (col, *peers):
+            for r, source, target in ((up, 0, 8 + CR), (down, CR - 8, 0)):
+                copies.append(
+                    send(
+                        heat_own.at[phase, pl.ds(source, 8), :],
+                        heat_all.at[phase, col, pl.ds(target, 8), :],
+                        (r, c),
+                    )
+                )
+        return copies
+
+    tall = (CR + 8) // 8
+
+    def thermal_coefs(place):
+        low = jnp.logical_and(place == 3, col == 0)
+        high = jnp.logical_and(place == GL + 2, col == NC - 1)
+        for i in range(tall):
             rows = pl.ds(8 * i, 8)
-            centers = [lat[layer, t, pl.ds(8 + 8 * i, 8), :] for t in range(NC)]
+            centers = [lat[place + 1, t, pl.ds(8 + 8 * i, 8), :] for t in range(NC)]
             west, east = west_east(centers)
             for t in range(NC):
                 k, k_w, k_e = centers[t], west[t], east[t]
-                k_n = lat[layer, t, pl.ds(7 + 8 * i, 8), :]
-                k_s = lat[layer, t, pl.ds(9 + 8 * i, 8), :]
-                v = ver[layer + 1, t, rows, :]
-                v_b = jnp.where(low, 0.0, ver[layer, t, rows, :])
-                v_a = jnp.where(high, 0.0, ver[layer + 2, t, rows, :])
+                k_n = lat[place + 1, t, pl.ds(7 + 8 * i, 8), :]
+                k_s = lat[place + 1, t, pl.ds(9 + 8 * i, 8), :]
+                v = ver[place + 1, t, rows, :]
+                v_b = jnp.where(low, 0.0, ver[place, t, rows, :])
+                v_a = jnp.where(high, 0.0, ver[place + 2, t, rows, :])
                 edge_n = edge_s = edge_w = edge_e = None
                 if i == 0:
-                    edge_n = jnp.logical_and(sub == 0, row == 0)
+                    edge_n = jnp.logical_and(sub == 4, row == 0)
                     k_n = jnp.where(edge_n, 0.0, k_n)
-                if i == CR // 8 - 1:
-                    edge_s = jnp.logical_and(sub == 7, row == NR - 1)
+                if i == tall - 1:
+                    edge_s = jnp.logical_and(sub == 3, row == NR - 1)
                     k_s = jnp.where(edge_s, 0.0, k_s)
                 if t == 0:
                     edge_w = first_lane
@@ -396,47 +414,39 @@
                 sums = [k + k_n, k + k_s, k + k_w, k + k_e, v + v_b, v + v_a]
                 twice = ((sums[0] + sums[1]) + (sums[2] + sums[3])) + (sums[4] + sums[5])
                 inverse = reciprocal(twice)
-                t_r[layer, t, rows, :] = 2.0 * inverse
+                t_r[place, t, rows, :] = 2.0 * inverse
                 edges = (edge_n, edge_s, edge_w, edge_e, low, high)
                 for ref, total, edge in zip((t_n, t_s, t_w, t_e, t_b, t_a), sums, edges):
                     value = total * inverse
                     if edge is not None:
                         value = jnp.where(edge, 0.0, value)
-                    ref[layer, t, rows, :] = value
+                    ref[place, t, rows, :] = value
+
+    def over(first, last, body):
+        def over_body(j, carry):
+            body(j)
+            return carry
+
+        lax.fori_loop(first, last, over_body, 0)
 
     def sources(phase, start):
-        def source_body(layer, carry):
-            for i in range(CR // 8):
+        def source_layer(place):
+            for i in range(tall):
                 rows = pl.ds(8 * i, 8)
+                near_rows = pl.ds(4 + 8 * i, 8)
                 for t in range(NC):
-                    here = layers[t, rows, :] == col * GL + layer
+                    here = layers[t, near_rows, :] == col * GL + place - 3
                     value = (
-                        jnp.where(here, heat_all[phase, t, rows, :], 0.0) * t_r[layer, t, rows, :]
+                        jnp.where(here, heat_all[phase, t, near_rows, :], 0.0)
+                        * t_r[place, t, rows, :]
                     )
-                    b_t[layer, t, rows, :] = value
+                    b_t[place, t, rows, :] = value
                     if start:
-                        temp_0[layer + 1, t, pl.ds(8 + 8 * i, 8), :] = value
-            return carry
-
-        lax.fori_loop(0, GL, source_body, 0)
-        if start:
-            for side, target, layer in ((0, 0, -1), (1, GL + 1, GL)):
-                for i in range(CR // 8):
-                    rows = pl.ds(8 * i, 8)
-                    for t in range(NC):
-                        here = layers[t, rows, :] == col * GL + layer
-                        temp_0[target, t, pl.ds(8 + 8 * i, 8), :] = (
-                            jnp.where(here, heat_all[phase, t, rows, :], 0.0)
-                            * r_far[side, t, rows, :]
-                        )
-
-    half = NC // 2
-    chunks = (range(half), range(half, NC))
-    tall = CR // 8
-    edge_tiles = sorted({0, tall - 1})
-    mid_tiles = [i for i in range(tall) if i not in edge_tiles]
-
-    def thermal_block(src, dst, first, depth, row_tiles, tiles, out=None):
+                        temp_0[place + 1, t, pl.ds(8 + 8 * i, 8), :] = value
+
+        over(0, GL + 6, source_layer)
+
+    def thermal_block(src, dst, first, depth):
         cache = {}
 
         def at(k, i, t):
@@ -444,155 +454,59 @@
                 cache[k, i, t] = src[first + k, t, pl.ds(8 + 8 * i, 8), :]
             return cache[k, i, t]
 
-        for k in range(depth):
-            layer = first + k
-            for i in row_tiles:
-                rows = pl.ds(8 * i, 8)
-                plus = {
-                    t: pltpu.roll(at(k + 1, i, t), 1, axis=1)
-                    for t in range(max(tiles[0] - 1, 0), tiles[-1] + 1)
-                }
-                minus = {
-                    t: pltpu.roll(at(k + 1, i, t), 127, axis=1)
-                    for t in range(tiles[0], min(tiles[-1] + 2, NC))
-                }
-                for t in tiles:
+        for i in range(tall):
+            rows = pl.ds(8 * i, 8)
+            for k in range(depth):
+                place = first + k
+                plus = [pltpu.roll(at(k + 1, i, t), 1, axis=1) for t in range(NC)]
+                minus = [pltpu.roll(at(k + 1, i, t), 127, axis=1) for t in range(NC)]
+                for t in range(NC):
                     west = plus[t] if t == 0 else jnp.where(first_lane, plus[t - 1], plus[t])
                     east = minus[t] if t == NC - 1 else jnp.where(last_lane, minus[t + 1], minus[t])
-                    value = (
+                    dst[place + 1, t, pl.ds(8 + 8 * i, 8), :] = (
                         (
-                            b_t[layer, t, rows, :]
-                            + t_n[layer, t, rows, :] * src[layer + 1, t, pl.ds(7 + 8 * i, 8), :]
+                            b_t[place, t, rows, :]
+                            + t_n[place, t, rows, :] * src[place + 1, t, pl.ds(7 + 8 * i, 8), :]
                         )
                         + (
-                            t_s[layer, t, rows, :] * src[layer + 1, t, pl.ds(9 + 8 * i, 8), :]
-                            + t_b[layer, t, rows, :] * at(k, i, t)
+                            t_s[place, t, rows, :] * src[place + 1, t, pl.ds(9 + 8 * i, 8), :]
+                            + t_b[place, t, rows, :] * at(k, i, t)
                         )
-                        + (t_a[layer, t, rows, :] * at(k + 2, i, t))
-                        + (t_w[layer, t, rows, :] * west + t_e[layer, t, rows, :] * east)
+                        + (t_a[place, t, rows, :] * at(k + 2, i, t))
+                        + (t_w[place, t, rows, :] * west + t_e[place, t, rows, :] * east)
                     )
-                    if out is None:
-                        dst[layer + 1, t, pl.ds(8 + 8 * i, 8), :] = value
-                    else:
-                        out[layer, rows, 128 * t : 128 * t + 128] = value
-
-    def inner_layers(src, dst, row_tiles, out=None):
-        depth = (GL - 2) // 2
-
-        def inner_body(j, carry):
-            thermal_block(src, dst, 1 + depth * j, depth, row_tiles, range(NC), out)
-            return carry
-
-        if row_tiles:
-            lax.fori_loop(0, 2, inner_body, 0)
-
-    def send_planes(ref, chunk):
-        mid, tiles = pl.ds(8, CR), pl.ds(chunk[0], len(chunk))
-        return [
-            send(ref.at[GL, tiles, mid, :], ref.at[0, tiles, mid, :], (row, right)),
-            send(ref.at[1, tiles, mid, :], ref.at[GL + 1, tiles, mid, :], (row, left)),
-        ]
-
-    def send_rims(ref, level):
-        def rim_body(layer, carry):
-            for t in range(NC):
-                rim_send[level - 1, 0, t, pl.ds(layer, 1), :] = ref[layer + 1, t, pl.ds(8, 1), :]
-                rim_send[level - 1, 1, t, pl.ds(layer, 1), :] = ref[
-                    layer + 1, t, pl.ds(7 + CR, 1), :
-                ]
-            return carry
-
-        lax.fori_loop(0, GL, rim_body, 0)
-        return [
-            send(rim_send.at[level - 1, side], rim_recv.at[level - 1, side], (r, col))
-            for side, r in ((0, up), (1, down))
-        ]
-
-    def place_rims(ref, level):
-        def place_body(layer, carry):
-            for t in range(NC):
-                ref[layer + 1, t, pl.ds(8 + CR, 1), :] = rim_recv[
-                    level - 1, 0, t, pl.ds(layer, 1), :
-                ]
-                ref[layer + 1, t, pl.ds(7, 1), :] = rim_recv[level - 1, 1, t, pl.ds(layer, 1), :]
-            return carry
-
-        lax.fori_loop(0, GL, place_body, 0)
-
-    def faces(body):
-        def face_body(j, carry):
-            body(j * (GL - 1))
-            return carry
-
-        lax.fori_loop(0, 2, face_body, 0)
-
-    def interior(body):
-        def interior_body(j, carry):
-            body(j)
-            return carry
-
-        lax.fori_loop(1, GL - 1, interior_body, 0)
+
+    def thermal_sweep(src, dst, halo):
+        over(
+            0,
+            GL // 2 + halo,
+            lambda j: thermal_block(src, dst, 3 - halo + 2 * j, 2),
+        )
 
     power_coefs(p_cond, True)
-    loaded(5, ver.at[pl.ds(1, GL)])
-    loaded(6, layers)
-    for copy in ver_copies + lat_copies:
-        copy.wait_recv()
-    faces(thermal_coefs)
-    r_copies = [
-        send(t_r.at[GL - 1], r_far.at[0], (row, right)),
-        send(t_r.at[0], r_far.at[1], (row, left)),
-    ]
     power_sweep(b_p, d_0)
     power_sweep(d_0, d_1)
     power_sweep(d_1, d_0)
     heat_copies = send_heat(p_cond, d_0, d_1, 0)
-    interior(thermal_coefs)
-    for copy in heat_copies + r_copies:
+    for copy in lat_copies + ver_copies:
+        copy.wait_recv()
+    over(0, GL + 6, thermal_coefs)
+    for copy in heat_copies + layer_copies:
         copy.wait_recv()
     sources(0, True)
-    pending = list(row_copies + col_copies + ver_copies + lat_copies + r_copies + heat_copies)
-
-    rims = {1: send_rims(temp_0, 1)}
-    planes = {}
-
-    def sweep(level, exchange=True, out=None):
-        src, dst = (temp_0, temp_1) if level % 2 == 0 else (temp_1, temp_0)
-        for copies in planes.get(level - 2, ()):
-            for copy in copies:
-                copy.wait_send()
-        for copy in rims[level - 1]:
-            copy.wait_recv()
-        place_rims(src, level - 1)
-        sent = []
-        for index, chunk in enumerate(chunks):
-            if level - 1 in planes:
-                for copy in planes[level - 1][index]:
-                    copy.wait_recv()
-            for layer in (0, GL - 1):
-                thermal_block(src, dst, layer, 1, range(tall), chunk, out)
-            if exchange:
-                sent.append(send_planes(dst, chunk))
-        if exchange:
-            planes[level] = sent
-            inner_layers(src, dst, edge_tiles)
-            rims[level] = send_rims(dst, level)
-            inner_layers(src, dst, mid_tiles)
-        else:
-            inner_layers(src, dst, list(range(tall)), out)
-
-    sweep(2)
-    sweep(3)
-    sweep(4, False)
+    pending = row_copies + col_copies + lat_copies + ver_copies + layer_copies + heat_copies
+    thermal_sweep(temp_0, temp_1, 2)
+    thermal_sweep(temp_1, temp_0, 1)
+    thermal_sweep(temp_0, temp_1, 0)
 
     def part_body(i, carry):
         base = pl.multiple_of(8 * i, 8)
         for t in range(NC):
-            ids = layers[t, pl.ds(base, 8), :] - col * GL
+            ids = layers[t, pl.ds(8 + base, 8), :] - col * GL
             total = jnp.zeros((8, 128), F32)
             for layer in range(GL):
                 total = jnp.where(
-                    ids == layer, temp_1[layer + 1, t, pl.ds(8 + base, 8), :], total
+                    ids == layer, temp_1[layer + 4, t, pl.ds(12 + base, 8), :], total
                 )
             part[t, pl.ds(base, 8), :] = total
         return carry
@@ -601,8 +515,6 @@
     part_copies = [
         send(part.at[peer], part_recv.at[k], (row, peer)) for k, peer in enumerate(peers)
     ]
-    rims[4] = send_rims(temp_1, 4)
-    planes[4] = [send_planes(temp_1, chunk) for chunk in chunks]
     for copy in part_copies:
         copy.wait_recv()
     total = part[col]
@@ -664,6 +576,7 @@
 
     lax.fori_loop(0, TR // 16 + 1, warm_side_body, 0)
 
+    temp_copies = send_rim(temp_1, 12, 4)
     power_coefs(c_now, False)
     power_sweep(d_0, d_1)
     power_sweep(d_1, d_0)
@@ -673,17 +586,21 @@
     for copy in heat_copies:
         copy.wait_recv()
     sources(1, False)
-    pending += part_copies + cell_copies + heat_copies
-    sweep(5)
-    sweep(6)
-    sweep(7)
-    sweep(8, False, temp_out)
-    for copies in rims.values():
-        pending += copies
-    for copies in planes[7]:
-        pending += copies
-    for copy in pending:
+    for copy in temp_copies:
+        copy.wait()
+    thermal_sweep(temp_1, temp_0, 3)
+    thermal_sweep(temp_0, temp_1, 2)
+    thermal_sweep(temp_1, temp_0, 1)
+    thermal_sweep(temp_0, temp_1, 0)
+    for t in range(NC):
+        pltpu.make_async_copy(
+            temp_1.at[pl.ds(4, GL), t, pl.ds(12, CR), :],
+            temp_out.at[:, :, pl.ds(128 * t, 128)],
+            load_sem.at[11],
+        ).start()
+    for copy in pending + part_copies + cell_copies + heat_copies:
         copy.wait_send()
+    loaded(11, temp_1.at[pl.ds(4, GL), :, pl.ds(12, CR), :])
 
 
 def body(num_rows, num_cols, demand, leakage, conductance, vias, layer_of, lateral_k, vertical_k):
@@ -691,7 +608,7 @@
     group_layers, cell_rows, therm_cols = lateral_k.shape
     sizes = (num_rows, num_cols, tile_rows, group_layers, cell_rows)
     fine = pltpu.VMEM((9, tile_rows + 48, 128), F32)
-    slab = pltpu.VMEM((group_layers, num_cols, cell_rows, 128), F32)
+    slab = pltpu.VMEM((group_layers + 6, num_cols, cell_rows + 8, 128), F32)
     coarse = (cell_rows, 128)
     hbm = pl.BlockSpec(memory_space=pl.ANY)
     return pl.pallas_call(
@@ -701,7 +618,7 @@
             jax.ShapeDtypeStruct(lateral_k.shape, F32),
         ),
         in_specs=[hbm] * 7,
-        out_specs=(pl.BlockSpec(memory_space=pltpu.VMEM),) * 2,
+        out_specs=(pl.BlockSpec(memory_space=pltpu.VMEM), hbm),
         scratch_shapes=[fine] * 3
         + [pltpu.VMEM((9, tile_rows + 48, 128), jnp.int32)]
         + [fine] * 9
@@ -712,33 +629,30 @@
             pltpu.VMEM((tile_rows // 4, 128), F32),
             pltpu.VMEM((tile_rows // 4 + 16, 128), F32),
             pltpu.VMEM((tile_rows // 4 + 16, 128), F32),
-            pltpu.VMEM((num_cols,) + coarse, jnp.int32),
-            pltpu.VMEM((group_layers, num_cols, cell_rows + 16, 128), F32),
-            pltpu.VMEM((group_layers + 2, num_cols, cell_rows, 128), F32),
+            pltpu.VMEM((num_cols, cell_rows + 16, 128), jnp.int32),
+            pltpu.VMEM((group_layers + 8, num_cols, cell_rows + 24, 128), F32),
+            pltpu.VMEM((group_layers + 8, num_cols, cell_rows + 8, 128), F32),
         ]
         + [slab] * 8
         + [
-            pltpu.VMEM((2, num_cols) + coarse, F32),
-            pltpu.VMEM((group_layers + 2, num_cols, cell_rows + 16, 128), F32),
-            pltpu.VMEM((group_layers + 2, num_cols, cell_rows + 16, 128), F32),
+            pltpu.VMEM((group_layers + 8, num_cols, cell_rows + 24, 128), F32),
+            pltpu.VMEM((group_layers + 8, num_cols, cell_rows + 24, 128), F32),
             pltpu.VMEM((tile_cols, 128), BF16),
             pltpu.VMEM((8, 128, 128), BF16),
             pltpu.VMEM((cell_rows, tile_cols), F32),
-            pltpu.VMEM((7, 2, num_cols, group_layers, 128), F32),
-            pltpu.VMEM((7, 2, num_cols, group_layers, 128), F32),
             pltpu.VMEM((2,) + coarse, F32),
-            pltpu.VMEM((2, num_cols) + coarse, F32),
+            pltpu.VMEM((2, num_cols, cell_rows + 16, 128), F32),
             pltpu.VMEM((num_cols,) + coarse, F32),
             pltpu.VMEM((num_cols - 1,) + coarse, F32),
             pltpu.VMEM((3, cell_rows + 16, 128), F32),
             pltpu.VMEM((9, cell_rows + 16, 128), F32),
             pltpu.VMEM((9, cell_rows + 16, 128), F32),
-            pltpu.SemaphoreType.DMA((11,)),
+            pltpu.SemaphoreType.DMA((12,)),
             pltpu.SemaphoreType.DMA((LINKS,)),
             pltpu.SemaphoreType.DMA((LINKS,)),
         ],
         compiler_params=pltpu.CompilerParams(
-            collective_id=0, has_side_effects=True, vmem_limit_bytes=52 << 20
+            collective_id=0, has_side_effects=True, vmem_limit_bytes=58 << 20
         ),
         name="coupled",
     )(demand, leakage, conductance, vias, layer_of, lateral_k, vertical_k)

time: 93.4 us -> 103 us (1.10)
  the two profiles are of different devices: /device:TPU:8 before, /device:TPU:0 now
where the time goes in v3:
time: 103 us
  Pallas kernels  99 us (96%)
  local copies, waits for them, and re-layouts  3.37 us (3%)
    pallas_call x1, Pallas kernels, body(): pl.pallas_call(functools.partial(kernel, sizes), out_shape=(jax.ShapeDtyp...  99 us
    unnamed x4, local copies, waits for them, and re-layouts  3.37 us

profile of v3, /device:TPU:0, one launch (start us, length us, event | category | flops | bytes accessed | tf_op | source)
XLA Modules:
  0.0 103.0 jit_solution(14669077723619004449)
XLA Ops:
  0.6 99.0 %coupled.1 = (f32[256,1024]{1,0:T(8,128)}, f32[8,32,1024]{2,1,0:T(8,128)}) custom-call(f32[256,1024]{1,0:T(8,128)} %demand.1, f32[256,1024]{1,0:T(8,128)} %leakage.1, f32[256,1024]{1,0:T(8,128)} %conductance.1, s32[256,1024]{1,0:T(8,128)} %vias.1, s32[32,1024]{1,0:T(8,128)} %layer_of.1, f32[8,32,1024]{2,1,0:T(8,128)} %lateral.1, f32[8,32,1024]{2,1,0:T(8,128)} %vertical.1), custom_call_target="tpu_custom_call" | custom-call | tf_op jit(solution)/shard_map/coupled/pallas_call | solution.py:614
  99.6 0.0 copy-start
  99.6 2.4 %copy.11 = f32[256,1024]{1,0:T(8,128)} copy(f32[256,1024]{1,0:T(8,128)} %get-tuple-element.4) | data formatting | bytes 2097152
  102.0 0.0 copy-done
  102.0 1.0 copy.12
Async XLA Ops:
  99.6 2.4 %copy-start = (f32[8,32,1024]{2,1,0:T(8,128)S(1)}, f32[8,32,1024]{2,1,0:T(8,128)}, u32[]{:S(2)}) copy-start(f32[8,32,1024]{2,1,0:T(8,128)} %get-tuple-element.5) | copy-start | bytes 3145732

commit v4 on v2

--- a/solution.py
+++ b/solution.py
@@ -17,7 +17,7 @@
 MESH = pl.DeviceIdType.MESH
 F32 = jnp.float32
 BF16 = jnp.bfloat16
-LINKS = 128
+LINKS = 160
 COEF_TILES = 4
 HALVES = 2
 
@@ -87,6 +87,8 @@
     rows_sum,
     rim_send,
     rim_recv,
+    face_send,
+    face_recv,
     heat_own,
     heat_all,
     part,
@@ -164,14 +166,6 @@
     def loaded(index, ref):
         pltpu.make_async_copy(ref, ref, load_sem.at[index]).wait()
 
-    pl.semaphore_wait(barrier, len(near))
-
-    row_copies = []
-    for index, src in enumerate((conductance, demand, leakage, vias)):
-        for side, start, device in ((0, TR - 8, (down, col)), (1, 0, (up, col))):
-            dst = stage_i.at[side] if index == 3 else stage.at[side, index]
-            row_copies.append(send(src.at[pl.ds(start, 8), :], dst, device))
-
     for index, (_, dst) in enumerate(power):
         loaded(index, dst.at[pl.ds(0, 2), pl.ds(16, TR), :])
 
@@ -192,6 +186,14 @@
         return carry
 
     lax.fori_loop(0, TQ // 8, pack_body, 0)
+    pl.semaphore_wait(barrier, len(near))
+
+    row_copies = []
+    for index, src in enumerate((conductance, demand, leakage, vias)):
+        for side, start, device in ((0, TR - 8, (down, col)), (1, 0, (up, col))):
+            dst = stage_i.at[side] if index == 3 else stage.at[side, index]
+            row_copies.append(send(src.at[pl.ds(start, 8), :], dst, device))
+
     col_copies = []
     for src, dst, c in ((pl_send, pl_recv, left), (pr_send, pr_recv, right)):
         col_copies.append(send(src, dst.at[pl.ds(8, TQ), :], (row, c)))
@@ -493,31 +495,66 @@
             send(ref.at[1, tiles, mid, :], ref.at[GL + 1, tiles, mid, :], (row, left)),
         ]
 
-    def send_rims(ref, level):
+    def copy_rims(ref, level, layer_list, tiles, buffer, place, put):
+        for layer, slot in layer_list:
+            for t in tiles:
+                for side, inside, outside in ((0, 8, 8 + CR), (1, 7 + CR, 7)):
+                    if put:
+                        ref[layer + 1, t, pl.ds(outside, 1), :] = buffer[place(side, t, slot)]
+                    else:
+                        buffer[place(side, t, slot)] = ref[layer + 1, t, pl.ds(inside, 1), :]
+
+    def inner_rims(ref, level, buffer, put):
         def rim_body(layer, carry):
-            for t in range(NC):
-                rim_send[level - 1, 0, t, pl.ds(layer, 1), :] = ref[layer + 1, t, pl.ds(8, 1), :]
-                rim_send[level - 1, 1, t, pl.ds(layer, 1), :] = ref[
-                    layer + 1, t, pl.ds(7 + CR, 1), :
-                ]
+            copy_rims(
+                ref,
+                level,
+                ((layer, layer),),
+                range(NC),
+                buffer,
+                lambda side, t, slot: (level - 1, side, t, pl.ds(slot, 1), slice(None)),
+                put,
+            )
             return carry
 
-        lax.fori_loop(0, GL, rim_body, 0)
+        lax.fori_loop(1, GL - 1, rim_body, 0)
+
+    def face_rims(ref, level, index, buffer, put):
+        copy_rims(
+            ref,
+            level,
+            ((0, 0), (GL - 1, 1)),
+            chunks[index],
+            buffer,
+            lambda side, t, slot: (
+                level - 1,
+                side,
+                index,
+                t - chunks[index][0],
+                pl.ds(slot, 1),
+                slice(None),
+            ),
+            put,
+        )
+
+    def send_inner(ref, level):
+        inner_rims(ref, level, rim_send, False)
         return [
             send(rim_send.at[level - 1, side], rim_recv.at[level - 1, side], (r, col))
             for side, r in ((0, up), (1, down))
         ]
 
-    def place_rims(ref, level):
-        def place_body(layer, carry):
-            for t in range(NC):
-                ref[layer + 1, t, pl.ds(8 + CR, 1), :] = rim_recv[
-                    level - 1, 0, t, pl.ds(layer, 1), :
-                ]
-                ref[layer + 1, t, pl.ds(7, 1), :] = rim_recv[level - 1, 1, t, pl.ds(layer, 1), :]
-            return carry
-
-        lax.fori_loop(0, GL, place_body, 0)
+    def send_face(ref, level, index):
+        face_rims(ref, level, index, face_send, False)
+        cut = pl.ds(0, 2)
+        return [
+            send(
+                face_send.at[level - 1, side, index, :, cut, :],
+                face_recv.at[level - 1, side, index, :, cut, :],
+                (r, col),
+            )
+            for side, r in ((0, up), (1, down))
+        ]
 
     def faces(body):
         def face_body(j, carry):
@@ -553,7 +590,8 @@
     sources(0, True)
     pending = list(row_copies + col_copies + ver_copies + lat_copies + r_copies + heat_copies)
 
-    rims = {1: send_rims(temp_0, 1)}
+    face_copies = {1: [send_face(temp_0, 1, index) for index in range(2)]}
+    rims = {1: send_inner(temp_0, 1)}
     planes = {}
 
     def sweep(level, exchange=True, out=None):
@@ -561,22 +599,26 @@
         for copies in planes.get(level - 2, ()):
             for copy in copies:
                 copy.wait_send()
-        for copy in rims[level - 1]:
-            copy.wait_recv()
-        place_rims(src, level - 1)
-        sent = []
+        planes_now, faces_now = [], []
         for index, chunk in enumerate(chunks):
+            for copy in face_copies[level - 1][index]:
+                copy.wait_recv()
             if level - 1 in planes:
                 for copy in planes[level - 1][index]:
                     copy.wait_recv()
+            face_rims(src, level - 1, index, face_recv, True)
             for layer in (0, GL - 1):
                 thermal_block(src, dst, layer, 1, range(tall), chunk, out)
             if exchange:
-                sent.append(send_planes(dst, chunk))
+                planes_now.append(send_planes(dst, chunk))
+                faces_now.append(send_face(dst, level, index))
+        for copy in rims[level - 1]:
+            copy.wait_recv()
+        inner_rims(src, level - 1, rim_recv, True)
         if exchange:
-            planes[level] = sent
+            planes[level], face_copies[level] = planes_now, faces_now
             inner_layers(src, dst, edge_tiles)
-            rims[level] = send_rims(dst, level)
+            rims[level] = send_inner(dst, level)
             inner_layers(src, dst, mid_tiles)
         else:
             inner_layers(src, dst, list(range(tall)), out)
@@ -601,8 +643,6 @@
     part_copies = [
         send(part.at[peer], part_recv.at[k], (row, peer)) for k, peer in enumerate(peers)
     ]
-    rims[4] = send_rims(temp_1, 4)
-    planes[4] = [send_planes(temp_1, chunk) for chunk in chunks]
     for copy in part_copies:
         copy.wait_recv()
     total = part[col]
@@ -664,6 +704,9 @@
 
     lax.fori_loop(0, TR // 16 + 1, warm_side_body, 0)
 
+    planes[4] = [send_planes(temp_1, chunk) for chunk in chunks]
+    face_copies[4] = [send_face(temp_1, 4, index) for index in range(2)]
+    rims[4] = send_inner(temp_1, 4)
     power_coefs(c_now, False)
     power_sweep(d_0, d_1)
     power_sweep(d_1, d_0)
@@ -680,6 +723,9 @@
     sweep(8, False, temp_out)
     for copies in rims.values():
         pending += copies
+    for pair in face_copies.values():
+        for copies in pair:
+            pending += copies
     for copies in planes[7]:
         pending += copies
     for copy in pending:
@@ -726,6 +772,8 @@
             pltpu.VMEM((cell_rows, tile_cols), F32),
             pltpu.VMEM((7, 2, num_cols, group_layers, 128), F32),
             pltpu.VMEM((7, 2, num_cols, group_layers, 128), F32),
+            pltpu.VMEM((7, 2, 2, num_cols // 2, 8, 128), F32),
+            pltpu.VMEM((7, 2, 2, num_cols // 2, 8, 128), F32),
             pltpu.VMEM((2,) + coarse, F32),
             pltpu.VMEM((2, num_cols) + coarse, F32),
             pltpu.VMEM((num_cols,) + coarse, F32),

time: 93.4 us -> 93.4 us (level)
  the two profiles are of different devices: /device:TPU:8 before, /device:TPU:0 now
where the time goes in v4:
time: 93.4 us; the launch traced here: 93.3 us
  Pallas kernels  89.1 us (95%)
  local copies, waits for them, and re-layouts  3.46 us (4%)
    pallas_call x1, Pallas kernels, body(): pl.pallas_call(functools.partial(kernel, sizes), out_shape=(jax.ShapeDtyp...  89.1 us
    unnamed x6, local copies, waits for them, and re-layouts  3.46 us

profile of v4, /device:TPU:0, one launch (start us, length us, event | category | flops | bytes accessed | tf_op | source)
XLA Modules:
  0.0 93.3 jit_solution(14677535643055130315)
XLA Ops:
  0.6 0.0 copy-start
  0.6 0.9 copy-done
  1.5 89.1 %coupled.1 = (f32[256,1024]{1,0:T(8,128)S(1)}, f32[8,32,1024]{2,1,0:T(8,128)}) custom-call(f32[256,1024]{1,0:T(8,128)} %demand.1, f32[256,1024]{1,0:T(8,128)} %leakage.1, f32[256,1024]{1,0:T(8,128)} %conductance.1, s32[256,1024]{1,0:T(8,128)} %vias.1, s32[32,1024]{1,0:T(8,128)S(1)} %copy-done, f32[8,32,1024]{2,1,0:T(8,128)} %lateral.1, f32[8,32,1024]{2,1,0:T(8,128)} %vertical.1), custom_call_target="tpu_custom_call" | custom-call | tf_op jit(solution)/shard_map/coupled/pallas_call | solution.py:743
  90.7 0.0 copy-start.1
  90.7 1.0 %copy.11 = f32[256,1024]{1,0:T(8,128)} copy(f32[256,1024]{1,0:T(8,128)S(1)} %get-tuple-element.4) | data formatting | bytes 2097152
  91.7 0.6 copy-done.1
  92.3 1.0 %copy.12 = f32[8,32,1024]{2,1,0:T(8,128)} copy(f32[8,32,1024]{2,1,0:T(8,128)S(1)} %copy-done.1) | data formatting | bytes 2097152
Async XLA Ops:
  0.6 0.9 copy-start
  90.7 1.6 %copy-start.1 = (f32[8,32,1024]{2,1,0:T(8,128)S(1)}, f32[8,32,1024]{2,1,0:T(8,128)}, u32[]{:S(2)}) copy-start(f32[8,32,1024]{2,1,0:T(8,128)} %get-tuple-element.5) | copy-start | bytes 3145732

commit v5 on v4

--- a/solution.py
+++ b/solution.py
@@ -145,7 +145,8 @@
 
     power = ((conductance, p_cond), (demand, p_dem), (leakage, p_leak), (vias, p_via))
     outer_tiles, inner_tiles = (0, NT - 1), tuple(range(1, NT - 1))
-    for offset, tiles in ((0, outer_tiles), (7, inner_tiles)):
+
+    def load_power(offset, tiles):
         for index, (src, dst) in enumerate(power):
             for t in tiles:
                 pltpu.make_async_copy(
@@ -153,6 +154,16 @@
                     dst.at[t, pl.ds(16, TR), :],
                     load_sem.at[offset + index],
                 ).start()
+    load_power(0, outer_tiles)
+    pl.semaphore_wait(barrier, len(near))
+
+    row_copies = []
+    for index, src in enumerate((conductance, demand, leakage, vias)):
+        for side, start, device in ((0, TR - 8, (down, col)), (1, 0, (up, col))):
+            dst = stage_i.at[side] if index == 3 else stage.at[side, index]
+            row_copies.append(send(src.at[pl.ds(start, 8), :], dst, device))
+
+    load_power(7, inner_tiles)
     for t in range(NC):
         cut = pl.ds(128 * t, 128)
         pltpu.make_async_copy(
@@ -186,14 +197,6 @@
         return carry
 
     lax.fori_loop(0, TQ // 8, pack_body, 0)
-    pl.semaphore_wait(barrier, len(near))
-
-    row_copies = []
-    for index, src in enumerate((conductance, demand, leakage, vias)):
-        for side, start, device in ((0, TR - 8, (down, col)), (1, 0, (up, col))):
-            dst = stage_i.at[side] if index == 3 else stage.at[side, index]
-            row_copies.append(send(src.at[pl.ds(start, 8), :], dst, device))
-
     col_copies = []
     for src, dst, c in ((pl_send, pl_recv, left), (pr_send, pr_recv, right)):
         col_copies.append(send(src, dst.at[pl.ds(8, TQ), :], (row, c)))

time: 93.4 us -> 95.8 us (1.026)
  Pallas kernels: 89.1 us -> 91.5 us
    pallas_call x1, Pallas kernels: 89.1 us -> 91.5 us  [body(): pl.pallas_call(functools.partial(kernel, sizes), out_shape=(jax.ShapeDtyp...]
where the time goes in v5:
time: 95.8 us; the launch traced here: 95.6 us
  Pallas kernels  91.5 us (96%)
  local copies, waits for them, and re-layouts  3.46 us (4%)
    pallas_call x1, Pallas kernels, body(): pl.pallas_call(functools.partial(kernel, sizes), out_shape=(jax.ShapeDtyp...  91.5 us
    unnamed x6, local copies, waits for them, and re-layouts  3.46 us

profile of v5, /device:TPU:0, one launch (start us, length us, event | category | flops | bytes accessed | tf_op | source)
XLA Modules:
  0.0 95.6 jit_solution(7343616411279304570)
XLA Ops:
  0.6 0.0 copy-start
  0.6 0.9 copy-done
  1.5 91.5 %coupled.1 = (f32[256,1024]{1,0:T(8,128)S(1)}, f32[8,32,1024]{2,1,0:T(8,128)}) custom-call(f32[256,1024]{1,0:T(8,128)} %demand.1, f32[256,1024]{1,0:T(8,128)} %leakage.1, f32[256,1024]{1,0:T(8,128)} %conductance.1, s32[256,1024]{1,0:T(8,128)} %vias.1, s32[32,1024]{1,0:T(8,128)S(1)} %copy-done, f32[8,32,1024]{2,1,0:T(8,128)} %lateral.1, f32[8,32,1024]{2,1,0:T(8,128)} %vertical.1), custom_call_target="tpu_custom_call" | custom-call | tf_op jit(solution)/shard_map/coupled/pallas_call | solution.py:746
  93.0 0.0 copy-start.1
  93.1 1.0 %copy.11 = f32[256,1024]{1,0:T(8,128)} copy(f32[256,1024]{1,0:T(8,128)S(1)} %get-tuple-element.4) | data formatting | bytes 2097152
  94.0 0.6 copy-done.1
  94.7 1.0 %copy.12 = f32[8,32,1024]{2,1,0:T(8,128)} copy(f32[8,32,1024]{2,1,0:T(8,128)S(1)} %copy-done.1) | data formatting | bytes 2097152
Async XLA Ops:
  0.6 0.9 copy-start
  93.0 1.6 %copy-start.1 = (f32[8,32,1024]{2,1,0:T(8,128)S(1)}, f32[8,32,1024]{2,1,0:T(8,128)}, u32[]{:S(2)}) copy-start(f32[8,32,1024]{2,1,0:T(8,128)} %get-tuple-element.5) | copy-start | bytes 3145732
